TPU v7x, 128 devices: a whole 4x4x4 slice. The times are simulated.
128 devices in a mesh: dp: 16 (over z_hi, x, core), tp: 8 (over y, z_lo).
Axes of the slice: x: 4, y: 4, z: 4 (z_hi: 2, z_lo: 2; z = z_hi * 2 + z_lo), core: 2. Of those that a mesh axis runs over, the one named last changes fastest.
Arguments:
- hidden: bfloat16 [16384, 8192], P('dp', 'tp'), may hold values from -6 to 6
- norm_gain: float32 [8192], replicated, may hold values from 0.1 to 1.9
- lengths: int32 [32], P('dp'), may hold values from 1 to 512, 12288 in all
- query_weight: bfloat16 [8192, 8192], P('dp', 'tp'), may hold values from -0.0625 to 0.0625
- keyval_weight: bfloat16 [8192, 8, 2, 128], P('dp', 'tp'), may hold values from -0.0625 to 0.0625
Outputs:
- attended: bfloat16 [16384, 8192], P('dp', 'tp')
Inputs may be any that keep to these rules, and one draw needn't show every extreme that they name: `lengths`: each rollout has 1 to 512 live tokens, they sum to 12288, and some rollout has exactly 512.
All inputs are finite; a program needn't handle non-finite values. No bound on the sum of `lengths` on one device may be relied on, other than what follows from the above.
Results may differ from a plain program's by a relative error of at most 0.0085.
Values may be sent and summed in bfloat16 or wider, within the bound.
No kernel may reach another device: no remote copies, remote signals or barrier semaphores. Data moves between devices by JAX's collectives and lax.ppermute only.
A program may use at most 128 MiB of HBM per device.

v0:
```python
import jax
import jax.numpy as jnp
from jax import lax
from jax.sharding import PartitionSpec as P


def add_rows(source, weights):
    flat_weights = weights.reshape(weights.shape[0], -1)
    return jnp.dot(source, flat_weights, preferred_element_type=jnp.float32)


def attend_one(query, keyval, length):
    keys = keyval[:, :, 0]
    values = keyval[:, :, 1]
    span = query.shape[0]
    scale = query.shape[-1] ** (-0.5)
    scores = jnp.einsum("qkgd,jkd->kgqj", query, keys, preferred_element_type=jnp.float32) * scale
    rowpos = lax.broadcasted_iota(jnp.int32, (span, span), 0)
    colpos = lax.broadcasted_iota(jnp.int32, (span, span), 1)
    allowed = (colpos <= rowpos) & (colpos < length)
    scores = jnp.where(allowed, scores, -jnp.inf)
    peak = jnp.max(scores, axis=-1, keepdims=True)
    expo = jnp.exp(scores - peak)
    probs = (expo / jnp.sum(expo, axis=-1, keepdims=True)).astype(jnp.bfloat16)
    mixed = jnp.einsum("kgqj,jkd->qkgd", probs, values, preferred_element_type=jnp.float32)
    return mixed.astype(jnp.bfloat16)


def local(hidden, norm_gain, lengths, query_weight, keyval_weight):
    whole_rows = lax.all_gather(hidden, "tp", axis=1, tiled=True)
    widened = whole_rows.astype(jnp.float32)
    meansq = jnp.mean(widened * widened, axis=-1, keepdims=True)
    normed = (widened * lax.rsqrt(meansq + 1e-05) * norm_gain).astype(jnp.bfloat16)
    row_count = normed.shape[0]
    kv_local = keyval_weight.shape[1]
    head_size = keyval_weight.shape[3]

    def add_single(weights):
        return add_rows(normed, weights)

    keyval = add_single(lax.all_gather(keyval_weight, "dp", axis=0, tiled=True))
    query = add_single(lax.all_gather(query_weight, "dp", axis=0, tiled=True))
    keyval = keyval.astype(jnp.bfloat16)
    query = query.astype(jnp.bfloat16)
    groups = query.shape[1] // (kv_local * head_size)
    seq_count = lengths.shape[0]
    span = row_count // seq_count
    query = query.reshape(seq_count, span, kv_local, groups, head_size)
    keyval = keyval.reshape(seq_count, span, kv_local, 2, head_size)
    mixed = lax.map(lambda item: attend_one(item[0], item[1], item[2]), (query, keyval, lengths))
    return mixed.reshape(row_count, kv_local * groups * head_size)


def solution(mesh):
    in_specs = (P("dp", "tp"), P(), P("dp"), P("dp", "tp"), P("dp", "tp", None, None))
    out_specs = P("dp", "tp")
    return jax.shard_map(local, mesh=mesh, in_specs=in_specs, out_specs=out_specs, check_vma=False)
```

profile of v0, /device:TPU:0, one launch (start us, length us, event | category | flops | bytes accessed | tf_op | source)
XLA Modules:
  0.0 563.6 jit_solution(16249076195801173163)
XLA Ops:
  6.5 0.7 all-gather.4.cloned.1.call-update
  7.3 0.7 all-gather.6.cloned.1.call-update
  8.1 0.7 all-gather.8.cloned.1.call-update
  8.8 328.5 %all-gather.4.cloned.1.call-done = bf16[1024,8192]{1,0:T(8,128)(2,1)} async-done(((bf16[1024,1024]{1,0:T(8,128)(2,1)}), bf16[1024,8192]{1,0:T(8,128)(2,1)}) %all-gather.4.cloned.1.call-update) | async-done | bytes 16777232 | tf_op jit(solution)/shard_map/all_gather | solution.py:30
  337.2 7.2 %fusion.15 = f32[1024]{0:T(1024)S(1)} fusion(bf16[1024,8192]{1,0:T(8,128)(2,1)} %all-gather.4.cloned.1.call-done), kind=kLoop, calls=%fused_computation.25 | loop fusion | flops 25164800 | bytes 16781312 | tf_op jit(solution)/shard_map/reduce_sum | solution.py:32
  344.4 52.3 %all-gather.6.cloned.1.call-done = bf16[8192,1,2,128]{3,2,1,0:T(2,128)(2,1)} async-done(((bf16[512,1,2,128]{3,2,1,0:T(2,128)(2,1)}), bf16[8192,1,2,128]{3,2,1,0:T(2,128)(2,1)}) %all-gather.6.cloned.1.call-update) | async-done | bytes 4194320 | tf_op jit(solution)/shard_map/all_gather | solution.py:41
  396.7 11.6 %fusion.26 = bf16[1024,256]{1,0:T(8,128)(2,1)S(1)} fusion(bf16[1024,8,2,128]{3,2,1,0:T(2,128)(2,1)} %bitcast.93, bf16[1024,8192]{1,0:T(8,128)(2,1)} %all-gather.4.cloned.1.call-done, f32[8192]{0:T(1024)S(1)} %copy-done, f32[1024]{0:T(1024)S(1)} %add_rsqrt_fusion), kind=kOutput, calls=%fused_computation.34 | convolution fusion | flops 4328783872 | bytes 21532672 | tf_op jit(solution)/shard_map/dot_general | solution.py:9
  408.4 99.7 %all-gather.8.cloned.1.call-done = bf16[8192,1024]{1,0:T(8,128)(2,1)} async-done(((bf16[512,1024]{1,0:T(8,128)(2,1)}), bf16[8192,1024]{1,0:T(8,128)(2,1)}) %all-gather.8.cloned.1.call-update) | async-done | bytes 16777232 | tf_op jit(solution)/shard_map/all_gather | solution.py:42
  508.1 22.1 %convert_bitcast_fusion = bf16[128,8,8,128]{3,1,2,0:T(8,128)(2,1)S(1)} fusion(bf16[8192,1024]{1,0:T(8,128)(2,1)} %all-gather.8.cloned.1.call-done, bf16[1024,8192]{1,0:T(8,128)(2,1)} %all-gather.4.cloned.1.call-done, f32[8192]{0:T(1024)S(1)} %copy-done, f32[1024]{0:T(1024)S(1)} %add_rsqrt_fusion), kind=kOutput, calls=%fused_computation.33 | convolution fusion | flops 17214472192 | bytes 35688448 | tf_op jit(solution)/shard_map/dot_general | solution.py:9
  530.3 2.0 copy.24
  532.2 21.4 %while.10 = (s32[]{:T(128)}, bf16[2,512,1,8,128]{4,3,1,0,2:T(8,128)(2,1)}, bf16[2,512,1,2,128]{4,3,1,0,2:T(2,128)(2,1)S(1)}, s32[2]{0:T(128)S(1)}, bf16[2,512,1,8,128]{4,3,1,0,2:T(8,128)(2,1)}, /*index=5*/s32[]{:T(128)}) while((s32[]{:T(128)}, bf16[2,512,1,8,128]{4,3,1,0,2:T(8,128)(2,1)}, bf16[2,512,1,2,128]{4,3,1,0,2:T(2,128)(2,1)S(1)}, ...), condition=%wide.region_4.5_spmd, body=%wide.region_1.4_spmd.sunk | while | flops 1099948544 | bytes 35997276 | solution.py:50
  533.8 1.3 constant_dynamic-slice_fusion.4
  535.1 1.6 fusion.39
  536.7 1.7 fusion.40
  538.4 2.7 fusion.41
  541.1 0.8 copy.45
  541.9 1.0 constant_dynamic-update-slice_fusion.2
  544.5 1.3 constant_dynamic-slice_fusion.4
  545.8 1.6 fusion.39
  547.4 1.7 fusion.40
  549.1 2.7 fusion.41
  551.8 0.8 copy.45
  552.5 1.0 constant_dynamic-update-slice_fusion.2
  553.6 3.5 copy.39
  (20 shorter events, 3.4 us)
Async XLA Ops:
  6.5 330.7 %all-gather.4.cloned.1.call-start = ((), (), s32[]{:S(2)}) async-start(), calls=%async_computation | async-start | bytes 18874368 | tf_op jit(solution)/shard_map/all_gather | solution.py:30
  7.3 389.5 %all-gather.6.cloned.1.call-start = ((), (), s32[]{:S(2)}) async-start(), calls=%async_computation.1 | async-start | bytes 4456448 | tf_op jit(solution)/shard_map/all_gather | solution.py:41
  8.0 500.1 %all-gather.8.cloned.1.call-start = ((), (), s32[]{:S(2)}) async-start(), calls=%async_computation.2 | async-start | bytes 17825792 | tf_op jit(solution)/shard_map/all_gather | solution.py:42
  8.7 388.0 %copy-start = (f32[8192]{0:T(1024)S(1)}, f32[8192]{0:T(1024)}, u32[]{:S(2)}) copy-start(f32[8192]{0:T(1024)} %param.8) | copy-start | bytes 98308
  408.4 123.8 %copy-start.1 = (s32[2]{0:T(128)S(1)}, s32[2]{0:T(128)}, u32[]{:S(2)}) copy-start(s32[2]{0:T(128)} %param.9) | copy-start | bytes 28
Sparse Core Ops, SparseCore 0:
  9.0 328.1 all-gather.3
  339.7 56.9 all-gather.5
  399.2 108.8 all-gather.7
where the time goes:
time: 565 us; the launch traced here: 564 us
  waiting for transfers between devices  483 us (85%)
  matrix products  42.2 us (7%)
  local copies, waits for them, and re-layouts  13.4 us (2%)
  between operations  13.2 us (2%)
  other arithmetic  12.2 us (2%)
    all_gather x1, waiting for transfers between devices, local(): whole_rows = lax.all_gather(hidden, 'tp', axis=1, tiled=True)  328 us
    all_gather x1, waiting for transfers between devices, local(): query = add_single(lax.all_gather(query_weight, 'dp', axis=0, tiled=True))  99.7 us
    all_gather x1, waiting for transfers between devices, local(): keyval = add_single(lax.all_gather(keyval_weight, 'dp', axis=0, tiled=True))  52.3 us
    dot_general x2, matrix products, add_rows(): return jnp.dot(source, flat_weights, preferred_element_type=jnp.float32)  33.7 us
  transfers between devices with their start and end apart: 3, of which 3 were waited for; matrix products, arithmetic and copies ran while one was open for 3% of the time, Pallas kernels for 0%

commit v1 on v0

v1 whole, which is shorter than its diff:
```python
import jax
import jax.numpy as jnp
from jax import lax
from jax.experimental import pallas as pl
from jax.experimental.pallas import tpu as pltpu
from jax.sharding import Mesh, PartitionSpec as P

LOG2E = 1.4426950408889634
HEAD = 128
GROUPS = 8
EPS = 1e-05


def ring(a, axis, sign=1):
    perm = []
    for c in range(2):
        for i in range(4):
            j = (i + sign) % 4 if c == 0 else (i - sign) % 4
            if axis == "y":
                perm.append((c * 4 + i, c * 4 + j))
            else:
                perm.append((i * 2 + c, j * 2 + c))
    return lax.ppermute(a, ("c", "y") if axis == "y" else ("x", "c"), perm)


def swap(a, axis):
    return lax.ppermute(a, axis, [(0, 1), (1, 0)])


def flip(a, axis, bit):
    size = 4 if axis == "y" else 2
    return lax.ppermute(a, axis, [(i, i ^ bit) for i in range(size)])


def together(*arrays):
    return lax.optimization_barrier(arrays)


def attend_block(acc, inv, length, out_ref):
    span = acc.shape[0]
    half = span // 2
    factor = LOG2E * HEAD**-0.5
    at_k, at_v = GROUPS * HEAD, (GROUPS + 1) * HEAD
    k = (acc[:, at_k : at_k + HEAD] * inv).astype(jnp.bfloat16)
    v = (acc[:, at_v : at_v + HEAD] * inv).astype(jnp.bfloat16)
    v = jnp.concatenate([v, jnp.ones_like(v)], axis=1)
    for part in range(2):
        lo, hi = part * half, (part + 1) * half
        row = lax.broadcasted_iota(jnp.int32, (half, hi), 0) + lo
        col = lax.broadcasted_iota(jnp.int32, (half, hi), 1)
        bias = jnp.where((col <= row) & (col < length), 0.0, -jnp.inf)
        for g in range(GROUPS):
            at = slice(g * HEAD, (g + 1) * HEAD)
            q = (acc[lo:hi, at] * inv[lo:hi]).astype(jnp.bfloat16)
            s = lax.dot_general(
                q, k[:hi], (((1,), (1,)), ((), ())), preferred_element_type=jnp.float32
            )
            s = s + bias
            peak = jnp.max(s, axis=-1, keepdims=True)
            e = jnp.exp2((s - peak) * factor).astype(jnp.bfloat16)
            mixed = jnp.dot(e, v[:hi], preferred_element_type=jnp.float32)
            out_ref[lo:hi, at] = (mixed[:, :HEAD] / mixed[:, HEAD:]).astype(jnp.bfloat16)


def stage(parts, sel, weights, acc_in=None, final=None):
    flat, where = [], []
    for part in parts:
        spots = []
        for array, row, count in part:
            known = [i for i, have in enumerate(flat) if have is array]
            if not known:
                flat.append(array)
            spots.append((known[0] if known else len(flat) - 1, row, count))
        where.append(spots)
    n = len(parts)
    rows = sum(count for _, _, count in where[0])
    feats = flat[0].shape[1]
    deep, width = weights[0].shape
    extra = [] if acc_in is None else [acc_in]
    if final is not None:
        inv, length, out_row, out_old = final
        extra += [inv, length] + ([] if out_old is None else [out_old])

    def body(sel_ref, *refs):
        refs = list(refs)
        pieces = [refs.pop(0) for _ in flat]
        blocks = [refs.pop(0) for _ in weights]
        acc_ref = None if acc_in is None else refs.pop(0)
        if final is not None:
            inv_ref, length_ref = refs.pop(0), refs.pop(0)
            if out_old is not None:
                refs.pop(0)
        out_ref = refs.pop(0)
        a_buf, w_buf, acc, sem_a, sem_w, sem_c = refs[:6]

        def fetch(k, slot):
            for j, spots in enumerate(where):
                @pl.when(k == j)
                def _(spots=spots):
                    to = 0
                    for i, row, count in spots:
                        pltpu.make_async_copy(
                            pieces[i].at[pl.ds(row, count)], a_buf.at[slot, pl.ds(to, count)], sem_a.at[slot]
                        ).start()
                        to += count
            for side in range(2):
                for j, block in enumerate(blocks):
                    @pl.when(sel_ref[2 * k + side] == j)
                    def _(block=block, side=side):
                        pltpu.make_async_copy(
                            block, w_buf.at[slot, pl.ds(side * deep, deep)], sem_w.at[slot]
                        ).start()

        fetch(0, 0)
        if acc_ref is not None:
            load = pltpu.make_async_copy(acc_ref, acc, sem_c)
            load.start()
            load.wait()
        else:
            acc[...] = jnp.zeros_like(acc)

        def step(k, carry):
            slot = lax.rem(k, 2)

            @pl.when(k + 1 < n)
            def _():
                fetch(k + 1, 1 - slot)

            pltpu.make_async_copy(a_buf.at[slot], a_buf.at[slot], sem_a.at[slot]).wait()
            pltpu.make_async_copy(w_buf.at[slot], w_buf.at[slot], sem_w.at[slot]).wait()
            for tile in range(0, width, 256):
                at = slice(tile, tile + 256)
                acc[:, at] += jnp.dot(a_buf[slot], w_buf[slot, :, at], preferred_element_type=jnp.float32)
            return carry

        lax.fori_loop(0, n, step, 0)
        if final is None:
            save = pltpu.make_async_copy(acc, out_ref, sem_c)
        else:
            done = refs[6]
            attend_block(acc, inv_ref[...], length_ref[0], done)
            save = pltpu.make_async_copy(done, out_ref.at[pl.ds(out_row, rows)], sem_c)
        save.start()
        save.wait()

    anywhere = pl.BlockSpec(memory_space=pl.ANY)
    smem = pl.BlockSpec(memory_space=pltpu.SMEM)
    specs = [smem] + [anywhere] * (len(flat) + len(weights) + (acc_in is not None))
    scratch = [
        pltpu.VMEM((2, rows, feats), jnp.bfloat16),
        pltpu.VMEM((2, 2 * deep, width), jnp.bfloat16),
        pltpu.VMEM((rows, width), jnp.float32),
        pltpu.SemaphoreType.DMA((2,)),
        pltpu.SemaphoreType.DMA((2,)),
        pltpu.SemaphoreType.DMA,
    ]
    aliases = {}
    flops = 2 * n * rows * feats * width
    if final is None:
        out = jax.ShapeDtypeStruct((rows, width), jnp.float32)
    else:
        specs += [pl.BlockSpec(memory_space=pltpu.VMEM), smem]
        out = jax.ShapeDtypeStruct((2 * rows, GROUPS * HEAD), jnp.bfloat16)
        scratch.append(pltpu.VMEM((rows, GROUPS * HEAD), jnp.bfloat16))
        flops += 6 * 10**9
        if out_old is not None:
            aliases[len(specs)] = 0
            specs.append(anywhere)
    return pl.pallas_call(
        body,
        in_specs=specs,
        out_specs=anywhere,
        out_shape=out,
        scratch_shapes=scratch,
        input_output_aliases=aliases,
        compiler_params=pltpu.CompilerParams(vmem_limit_bytes=30 << 20),
        cost_estimate=pl.CostEstimate(flops=flops, bytes_accessed=n * 4 * 10**6, transcendentals=0),
    )(sel, *flat, *weights, *extra)


def local(hidden, norm_gain, lengths, query_weight, keyval_weight):
    zh, x, c = lax.axis_index("zh"), lax.axis_index("x"), lax.axis_index("c")
    y, zl = lax.axis_index("y"), lax.axis_index("zl")
    rows, feats = query_weight.shape[0], hidden.shape[1]
    span = hidden.shape[0] // 2
    cut = span + span // 2

    gain = lax.dynamic_slice(norm_gain, ((zh * 8 + x * 2 + c) * rows,), (rows,))
    own = jnp.concatenate([query_weight, keyval_weight.reshape(rows, -1)], axis=1)
    own = (own.astype(jnp.float32) * gain[:, None]).astype(jnp.bfloat16)
    width = own.shape[1]

    wide = hidden.astype(jnp.float32)
    square = jnp.sum(wide * wide, axis=-1).reshape(8, -1)
    square = square + flip(square, "y", 1)

    h0 = hidden
    far = swap(own, "zh")
    h1 = ring(h0, "y")
    w1, w3 = ring(own, "x"), ring(own, "x", -1)
    v0 = swap(own, "c")
    h0, w0, h1, w1, w3, f0, square = together(h0, own, h1, w1, w3, far, square)
    square = square + flip(square, "y", 2)
    h3 = ring(h0, "y", -1)
    lo0 = swap(h0[:span], "zl")
    w2, f1 = ring(w1, "x"), ring(f0, "x")
    v1, v3 = swap(w1, "c"), swap(w3, "c")
    h0, h1, h3, lo0, w2, f0, f1, square = together(h0, h1, h3, lo0, w2, f0, f1, square)
    square = square + flip(square, "zl", 1)
    h2a = ring(h1[:cut], "y")
    lo1 = ring(lo0, "y")
    hi0 = swap(h0[span:], "zl")
    f3, f2 = ring(f0, "x", -1), ring(f1, "x")
    v2, g0, g1 = swap(w2, "c"), swap(f0, "c"), swap(f1, "c")
    h1, h3, h2a, lo0, lo1, hi0, f3, f2 = together(h1, h3, h2a, lo0, lo1, hi0, f3, f2)
    g3, g2 = swap(f3, "c"), swap(f2, "c")
    lo2, lo3 = ring(lo1, "y"), ring(lo0, "y", -1)
    tails = swap(jnp.concatenate([h1[span:cut], h3[span:cut]], axis=0), "zl")
    weights = [w0, w1, w2, w3, v0, v1, v2, v3, f0, f1, f2, f3, g0, g1, g2, g3]
    half = span // 2

    def choose(*ones):
        step = jnp.array([k for k, _ in ones], jnp.int32)
        other = jnp.array([z for _, z in ones], jnp.int32)
        b = 2 * (jnp.where(c == 0, y - step, y + step) & 3) + (zl ^ other)
        z_at, x_at = b >> 2, b & 3
        core = jnp.array([0, 1], jnp.int32)[None, :]
        k = jnp.where(core == 0, x - x_at[:, None], x_at[:, None] - x) & 3
        return (((z_at ^ zh)[:, None]) * 8 + (core ^ c) * 4 + k).reshape(-1)

    first = [(h0, 0, span)], [(h1, 0, span)], [(h2a, 0, span)], [(h3, 0, span)], [(lo0, 0, span)], [(lo1, 0, span)]
    acc0 = stage(first, choose((0, 0), (1, 0), (2, 0), (3, 0), (0, 1), (1, 1)), weights)
    lo2, lo3, tails, h1, h2a, hi0, acc0 = together(lo2, lo3, tails, h1, h2a, hi0, acc0)
    h2b = ring(h1[cut:], "y")
    mid0 = hi0[half:]
    mid1, mid3 = ring(mid0, "y"), ring(mid0, "y", -1)
    tail2 = swap(h2a[span:], "zl")
    inv = lax.rsqrt(square.reshape(-1, 1) / (feats * 8) + EPS)
    out = stage(
        ([(lo2, 0, span)], [(lo3, 0, span)]), choose((2, 1), (3, 1)), weights, acc0, (inv[:span], lengths[:1], 0, None)
    )
    parts = [(h0, span, span)], [(h1, span, span)], [(h3, span, span)], [(hi0, 0, span)]
    acc1 = stage(parts, choose((0, 0), (1, 0), (3, 0), (0, 1)), weights)
    h2b, mid1, mid3, tail2, acc1, out = together(h2b, mid1, mid3, tail2, acc1, out)
    mid2 = ring(mid1, "y")
    parts = [(h2a, span, half), (h2b, 0, half)], [(tails, 0, half), (mid1, 0, half)], [(tails, half, half), (mid3, 0, half)]
    acc1 = stage(parts, choose((2, 0), (1, 1), (3, 1)), weights, acc1)
    parts = ([(tail2, 0, half), (mid2, 0, half)],)
    return stage(parts, choose((2, 1)), weights, acc1, (inv[span:], lengths[1:], span, out))


def solution(mesh):
    fine = Mesh(mesh.devices.reshape(2, 4, 2, 4, 2), ("zh", "x", "c", "y", "zl"))
    dp, tp = ("zh", "x", "c"), ("y", "zl")
    in_specs = (P(dp, tp), P(), P(dp), P(dp, tp), P(dp, tp, None, None))
    return jax.shard_map(local, mesh=fine, in_specs=in_specs, out_specs=P(dp, tp), check_vma=False)
```

time: 565 us -> 207 us (0.37)
  waiting for transfers between devices: 483 us -> 82.6 us
  Pallas kernels: 0 us -> 53.6 us
  starting transfers between devices: 0.08 us -> 44.5 us
  matrix products: 42.2 us -> 0 us
  between operations: 13.2 us -> 0.55 us
  other arithmetic: 12.2 us -> 3.48 us
  local copies, waits for them, and re-layouts: 13.4 us -> 19.8 us
    all_gather x3 -> x0, waiting for transfers between devices: 480 us -> none  [the longest x1 328 us: local(): whole_rows = lax.all_gather(hidden, 'tp', axis=1, tiled=True)]
    ppermute x0 -> x32, waiting for transfers between devices: none -> 82.6 us  [the longest x16 38.4 us: ring(): return lax.ppermute(a, ('c', 'y') if axis == 'y' else ('x', 'c'), perm)]
    pallas_call x0 -> x5, Pallas kernels: none -> 53.6 us  [stage(): pl.pallas_call(body, in_specs=specs, out_specs=anywhere, out_shape=out, s...]
    ppermute x0 -> x32, starting transfers between devices: none -> 44.5 us  [the longest x13 23.4 us: swap(): return lax.ppermute(a, axis, [(0, 1), (1, 0)])]
    dot_general x6 -> x0, matrix products: 42.2 us -> none  [the longest x2 33.7 us: add_rows(): return jnp.dot(source, flat_weights, preferred_element_type=jnp.float32)]
    reduce_sum x3 -> x1, other arithmetic: 10.6 us -> 0.48 us  [local(): square = jnp.sum(wide * wide, axis=-1).reshape(8, -1)]
    slice x0 -> x12, local copies, waits for them, and re-layouts: none -> 8.16 us  [the longest x2 2.15 us: local(): tails = swap(jnp.concatenate([h1[span:cut], h3[span:cut]], axis=0), 'zl')]
  transfers between devices with their start and end apart: 3 -> 32, of which waited for: 3 -> 12; matrix products, arithmetic and copies ran while one was open for 3% -> 7% of each run, Pallas kernels for 0% -> 22%
where the time goes in v1:
time: 207 us; the launch traced here: 205 us
  waiting for transfers between devices  82.6 us (40%)
  Pallas kernels  53.6 us (26%)
  starting transfers between devices  44.5 us (21%)
  local copies, waits for them, and re-layouts  19.8 us (10%)
  other arithmetic  3.48 us (2%)
    pallas_call x5, Pallas kernels, stage(): pl.pallas_call(body, in_specs=specs, out_specs=anywhere, out_shape=out, s...  53.6 us
    ppermute x16, waiting for transfers between devices, ring(): return lax.ppermute(a, ('c', 'y') if axis == 'y' else ('x', 'c'), perm)  38.4 us
    ppermute x13, waiting for transfers between devices, swap(): return lax.ppermute(a, axis, [(0, 1), (1, 0)])  27 us
    ppermute x13, starting transfers between devices, swap(): return lax.ppermute(a, axis, [(0, 1), (1, 0)])  23.4 us
    ppermute x16, starting transfers between devices, ring(): return lax.ppermute(a, ('c', 'y') if axis == 'y' else ('x', 'c'), perm)  17.8 us
    ppermute x3, waiting for transfers between devices, flip(): return lax.ppermute(a, axis, [(i, i ^ bit) for i in range(size)])  17.3 us
    unnamed x49, local copies, waits for them, and re-layouts  10.5 us
  transfers between devices with their start and end apart: 32, of which 12 were waited for; matrix products, arithmetic and copies ran while one was open for 7% of the time, Pallas kernels for 22%

profile of v1, /device:TPU:0, one launch (start us, length us, event | category | flops | bytes accessed | tf_op | source)
XLA Modules:
  0.0 204.6 jit_solution(10141600553654445565)
XLA Ops:
  0.0 1.7 collective-permute-start
  1.7 1.8 copy.26
  7.4 1.7 collective-permute-start.2
  9.2 3.9 %collective-permute-start.3 = (bf16[512,1280]{1,0:T(8,128)(2,1)S(1)}, bf16[512,1280]{1,0:T(8,128)(2,1)}, u32[]{:S(2)}, u32[]{:S(2)}) collective-permute-start(bf16[512,1280]{1,0:T(8,128)(2,1)S(1)} %multiply_convert_fusion.refs_6_.refs_4_.refs_2_.refs_5_), channel_id=1, source_target_pairs={{0,64},{64,0},{1,65},{65,1},{2,66},{66,2},{3,67},{67,3},{4,68},{68... | collective-permute-start | bytes 3932168 | tf_op jit(solution)/shard_map/ppermute | solution.py:27
  13.5 1.7 collective-permute-start.4
  15.2 10.4 %collective-permute-done.4 = f32[8,128]{1,0:T(8,128)S(1)} collective-permute-done((f32[8,128]{1,0:T(8,128)S(1)}, f32[8,128]{1,0:T(8,128)S(1)}, u32[]{:S(2)}, u32[]{:S(2)}) %collective-permute-start.4) | collective-permute-done | bytes 4128 | tf_op jit(solution)/shard_map/ppermute | solution.py:32
  25.6 10.7 %collective-permute-done.1.refs_7_.refs_5_.refs_3_.refs_6_ = bf16[512,1280]{1,0:T(8,128)(2,1)} collective-permute-done((bf16[512,1280]{1,0:T(8,128)(2,1)S(1)}, bf16[512,1280]{1,0:T(8,128)(2,1)}, u32[]{:S(2)}, u32[]{:S(2)}) %collective-permute-start.1) | collective-permute-done | bytes 1310752 | tf_op jit(solution)/shard_map/ppermute | solution.py:23
  37.9 4.4 %collective-permute-done.3.refs_14_.refs_12_.refs_10_.refs_13_ = bf16[512,1280]{1,0:T(8,128)(2,1)} collective-permute-done((bf16[512,1280]{1,0:T(8,128)(2,1)S(1)}, bf16[512,1280]{1,0:T(8,128)(2,1)}, u32[]{:S(2)}, u32[]{:S(2)}) %collective-permute-start.3) | collective-permute-done | bytes 1310752 | tf_op jit(solution)/shard_map/ppermute | solution.py:27
  46.8 4.9 %collective-permute-done.9 = f32[8,128]{1,0:T(8,128)S(1)} collective-permute-done((f32[8,128]{1,0:T(8,128)S(1)}, f32[8,128]{1,0:T(8,128)S(1)}, u32[]{:S(2)}, u32[]{:S(2)}) %collective-permute-start.9) | collective-permute-done | bytes 4128 | tf_op jit(solution)/shard_map/ppermute | solution.py:32
  51.7 14.6 %collective-permute-start.18 = (bf16[512,1280]{1,0:T(8,128)(2,1)S(1)}, bf16[512,1280]{1,0:T(8,128)(2,1)}, u32[]{:S(2)}, u32[]{:S(2)}) collective-permute-start(bf16[512,1280]{1,0:T(8,128)(2,1)S(1)} %multiply_convert_fusion.refs_6_.refs_4_.refs_2_.refs_5_), channel_id=1, source_target_pairs={{0,8},{8,0},{1,9},{9,1},{2,10},{10,2},{3,11},{11,3},{4,12},{12,4},... | collective-permute-start | bytes 3932168 | tf_op jit(solution)/shard_map/ppermute | solution.py:27
  67.4 10.3 %collective-permute-done.8.refs_15_.refs_13_.refs_11_.refs_14_ = bf16[512,1280]{1,0:T(8,128)(2,1)} collective-permute-done((bf16[512,1280]{1,0:T(8,128)(2,1)}, bf16[512,1280]{1,0:T(8,128)(2,1)}, u32[]{:S(2)}, u32[]{:S(2)}) %collective-permute-start.8) | collective-permute-done | bytes 1310752 | tf_op jit(solution)/shard_map/ppermute | solution.py:23
  85.4 15.8 %collective-permute-done.12.refs_3_ = bf16[512,1024]{1,0:T(8,128)(2,1)} collective-permute-done((bf16[512,1024]{1,0:T(8,128)(2,1)}, bf16[512,1024]{1,0:T(8,128)(2,1)}, u32[]{:S(2)}, u32[]{:S(2)}) %collective-permute-start.12) | collective-permute-done | bytes 1048608 | tf_op jit(solution)/shard_map/ppermute | solution.py:27
  101.4 13.4 %collective-permute-done.11.refs_5_ = bf16[512,1024]{1,0:T(8,128)(2,1)} collective-permute-done((bf16[512,1024]{1,0:T(8,128)(2,1)}, bf16[512,1024]{1,0:T(8,128)(2,1)}, u32[]{:S(2)}, u32[]{:S(2)}) %collective-permute-start.11) | collective-permute-done | bytes 1048608 | tf_op jit(solution)/shard_map/ppermute | solution.py:23
  118.4 2.0 collective-permute-done.30
  125.8 3.2 %collective-permute-start.16 = (bf16[512,1024]{1,0:T(8,128)(2,1)}, bf16[512,1024]{1,0:T(8,128)(2,1)}, u32[]{:S(2)}, u32[]{:S(2)}) collective-permute-start(bf16[512,1024]{1,0:T(8,128)(2,1)} %collective-permute-done.6.refs_4_), channel_id=1, source_target_pairs={{0,6},{2,0},{4,2},{6,4},{8,10},{10,12},{12,14},{14,8},{1,7},{3,1},... | collective-permute-start | bytes 3145736 | tf_op jit(solution)/shard_map/ppermute | solution.py:23
  130.6 14.1 %shard_map.190.refs_18_ = f32[512,1280]{1,0:T(8,128)} custom-call(s32[12]{0:T(128)S(1)} %add.188.sel_ref, bf16[1024,1024]{1,0:T(8,128)(2,1)} %refs_0_.1, bf16[1024,1024]{1,0:T(8,128)(2,1)} %collective-permute-done.refs_1_, bf16[768,1024]{1,0:T(8,128)(2,1)S(1)} %copy-done.6, bf16[1024,1024]{1,0:T(8,128)(2,1)} %copy-done.11, ...), custom_call_target="tpu_custom_call" | custom-call | flops 8053063680 | bytes 24000000 | tf_op jit(solution)/shard_map/pallas_call | solution.py:169
  144.7 5.6 %collective-permute-done.17.refs_2_ = bf16[512,1024]{1,0:T(8,128)(2,1)} collective-permute-done((bf16[512,1024]{1,0:T(8,128)(2,1)}, bf16[512,1024]{1,0:T(8,128)(2,1)}, u32[]{:S(2)}, u32[]{:S(2)}) %collective-permute-start.17) | collective-permute-done | bytes 1048608 | tf_op jit(solution)/shard_map/ppermute | solution.py:27
  150.3 2.3 %collective-permute-done.15.refs_0_ = bf16[512,1024]{1,0:T(8,128)(2,1)} collective-permute-done((bf16[512,1024]{1,0:T(8,128)(2,1)}, bf16[512,1024]{1,0:T(8,128)(2,1)}, u32[]{:S(2)}, u32[]{:S(2)}) %collective-permute-start.15) | collective-permute-done | bytes 1048608 | tf_op jit(solution)/shard_map/ppermute | solution.py:23
  153.8 3.2 %collective-permute-start.28 = (bf16[256,1024]{1,0:T(8,128)(2,1)S(1)}, bf16[256,1024]{1,0:T(8,128)(2,1)S(1)}, u32[]{:S(2)}, u32[]{:S(2)}) collective-permute-start(bf16[256,1024]{1,0:T(8,128)(2,1)S(1)} %slice.48), channel_id=1, source_target_pairs={{0,6},{2,0},{4,2},{6,4},{8,10},{10,12},{12,14},{14,8},{1,7},{3,1},... | collective-permute-start | bytes 1572872 | tf_op jit(solution)/shard_map/ppermute | solution.py:23
  159.0 10.8 %shard_map.192.refs_21_ = bf16[1024,1024]{1,0:T(8,128)(2,1)} custom-call(s32[4]{0:T(128)S(1)} %add.202.sel_ref, bf16[512,1024]{1,0:T(8,128)(2,1)} %collective-permute-done.15.refs_0_, bf16[512,1024]{1,0:T(8,128)(2,1)} %collective-permute-done.16.refs_1_, bf16[512,1280]{1,0:T(8,128)(2,1)S(1)} %multiply_convert_fusion.refs_6_.refs_4_.refs_2_.refs_5_, ...), custom_call_target="tpu_custom_call" | custom-call | flops 8684354560 | bytes 8000000 | tf_op jit(solution)/shard_map/pallas_call | solution.py:169
  169.9 10.2 %shard_map.191.refs_21_ = f32[512,1280]{1,0:T(8,128)} custom-call(s32[8]{0:T(128)S(1)} %add.195.sel_ref, bf16[1024,1024]{1,0:T(8,128)(2,1)S(1)} %copy-done.1, bf16[1024,1024]{1,0:T(8,128)(2,1)} %collective-permute-done.refs_1_, bf16[1024,1024]{1,0:T(8,128)(2,1)} %copy-done.11, bf16[512,1024]{1,0:T(8,128)(2,1)} %collective-permute-done.12.refs_3_, ...), custom_call_target="tpu_custom_call" | custom-call | flops 5368709120 | bytes 16000000 | tf_op jit(solution)/shard_map/pallas_call | solution.py:169
  184.2 9.7 %shard_map.193.refs_18_ = f32[512,1280]{1,0:T(8,128)} custom-call(s32[6]{0:T(128)S(1)} %add.212.sel_ref, bf16[768,1024]{1,0:T(8,128)(2,1)} %copy-done.5, bf16[256,1024]{1,0:T(8,128)(2,1)S(1)} %copy-done.10, bf16[512,1024]{1,0:T(8,128)(2,1)} %collective-permute-done.17.refs_2_, bf16[256,1024]{1,0:T(8,128)(2,1)} %collective-permute-done.27.refs_3_, ...), custom_call_target="tpu_custom_call" | custom-call | flops 4026531840 | bytes 12000000 | tf_op jit(solution)/shard_map/pallas_call | solution.py:169
  193.9 1.7 copy-done.4
  195.7 8.7 %shard_map.194 = bf16[1024,1024]{1,0:T(8,128)(2,1)} custom-call(s32[2]{0:T(128)S(1)} %and_add_fusion.4.sel_ref, bf16[256,1024]{1,0:T(8,128)(2,1)S(1)} %collective-permute-done.29.refs_0_, bf16[256,1024]{1,0:T(8,128)(2,1)} %collective-permute-done.31.refs_1_, ...), custom_call_target="tpu_custom_call", output_to_operand_aliasing={{}: (22, {})} | custom-call | flops 7342177280 | bytes 4000000 | tf_op jit(solution)/shard_map/pallas_call | solution.py:169
  (131 shorter events, 37.0 us)
Async XLA Ops:
  0.0 42.3 %collective-permute-start = (bf16[1024,1024]{1,0:T(8,128)(2,1)}, bf16[1024,1024]{1,0:T(8,128)(2,1)}, u32[]{:S(2)}, u32[]{:S(2)}) collective-permute-start(bf16[1024,1024]{1,0:T(8,128)(2,1)} %refs_0_.1), channel_id=1, source_target_pairs={{0,2},{2,4},{4,6},{6,0},{8,14},{10,8},{12,10},{14,12},{1,3},{3,5},... | collective-permute-start | bytes 6291464 | tf_op jit(solution)/shard_map/ppermute | solution.py:23
  5.9 30.5 %collective-permute-start.1 = (bf16[512,1280]{1,0:T(8,128)(2,1)S(1)}, bf16[512,1280]{1,0:T(8,128)(2,1)}, u32[]{:S(2)}, u32[]{:S(2)}) collective-permute-start(bf16[512,1280]{1,0:T(8,128)(2,1)S(1)} %multiply_convert_fusion.refs_6_.refs_4_.refs_2_.refs_5_), channel_id=1, source_target_pairs={{0,16},{16,32},{32,48},{48,0},{8,56},{24,8},{40,24},{56,40},{1,17}... | collective-permute-start | bytes 3932168 | tf_op jit(solution)/shard_map/ppermute | solution.py:23
  7.4 30.5 %collective-permute-start.2 = (bf16[512,1280]{1,0:T(8,128)(2,1)S(1)}, bf16[512,1280]{1,0:T(8,128)(2,1)S(1)}, u32[]{:S(2)}, u32[]{:S(2)}) collective-permute-start(bf16[512,1280]{1,0:T(8,128)(2,1)S(1)} %multiply_convert_fusion.refs_6_.refs_4_.refs_2_.refs_5_), channel_id=1, source_target_pairs={{0,48},{16,0},{32,16},{48,32},{8,24},{24,40},{40,56},{56,8},{1,49}... | collective-permute-start | bytes 3932168 | tf_op jit(solution)/shard_map/ppermute | solution.py:23
  9.2 33.2 %collective-permute-start.3 = (bf16[512,1280]{1,0:T(8,128)(2,1)S(1)}, bf16[512,1280]{1,0:T(8,128)(2,1)}, u32[]{:S(2)}, u32[]{:S(2)}) collective-permute-start(bf16[512,1280]{1,0:T(8,128)(2,1)S(1)} %multiply_convert_fusion.refs_6_.refs_4_.refs_2_.refs_5_), channel_id=1, source_target_pairs={{0,64},{64,0},{1,65},{65,1},{2,66},{66,2},{3,67},{67,3},{4,68},{68... | collective-permute-start | bytes 3932168 | tf_op jit(solution)/shard_map/ppermute | solution.py:27
  42.3 35.4 %collective-permute-start.5 = (bf16[1024,1024]{1,0:T(8,128)(2,1)S(1)}, bf16[1024,1024]{1,0:T(8,128)(2,1)S(1)}, u32[]{:S(2)}, u32[]{:S(2)}) collective-permute-start(bf16[1024,1024]{1,0:T(8,128)(2,1)S(1)} %copy-done), channel_id=1, source_target_pairs={{0,6},{2,0},{4,2},{6,4},{8,10},{10,12},{12,14},{14,8},{1,7},{3,1},... | collective-permute-start | bytes 6291464 | tf_op jit(solution)/shard_map/ppermute | solution.py:23
  43.1 24.2 %collective-permute-start.6 = (bf16[512,1024]{1,0:T(8,128)(2,1)S(1)}, bf16[512,1024]{1,0:T(8,128)(2,1)}, u32[]{:S(2)}, u32[]{:S(2)}) collective-permute-start(bf16[512,1024]{1,0:T(8,128)(2,1)S(1)} %slice.42), channel_id=1, source_target_pairs={{0,1},{1,0},{2,3},{3,2},{4,5},{5,4},{6,7},{7,6},{8,9},{9,8},{10,11... | collective-permute-start | bytes 3145736 | tf_op jit(solution)/shard_map/ppermute | solution.py:27
  44.5 22.9 %collective-permute-start.7 = (bf16[512,1280]{1,0:T(8,128)(2,1)}, bf16[512,1280]{1,0:T(8,128)(2,1)}, u32[]{:S(2)}, u32[]{:S(2)}) collective-permute-start(bf16[512,1280]{1,0:T(8,128)(2,1)} %collective-permute-done.1.refs_7_.refs_5_.refs_3_.refs_6_), channel_id=1, source_target_pairs={{0,16},{16,32},{32,48},{48,0},{8,56},{24,8},{40,24},{56,40},{1,17}... | collective-permute-start | bytes 3932168 | tf_op jit(solution)/shard_map/ppermute | solution.py:23
  45.0 32.7 %collective-permute-start.8 = (bf16[512,1280]{1,0:T(8,128)(2,1)}, bf16[512,1280]{1,0:T(8,128)(2,1)}, u32[]{:S(2)}, u32[]{:S(2)}) collective-permute-start(bf16[512,1280]{1,0:T(8,128)(2,1)} %collective-permute-done.3.refs_14_.refs_12_.refs_10_.refs_13_), channel_id=1, source_target_pairs={{0,16},{16,32},{32,48},{48,0},{8,56},{24,8},{40,24},{56,40},{1,17}... | collective-permute-start | bytes 3932168 | tf_op jit(solution)/shard_map/ppermute | solution.py:23
  51.7 32.0 %collective-permute-start.18 = (bf16[512,1280]{1,0:T(8,128)(2,1)S(1)}, bf16[512,1280]{1,0:T(8,128)(2,1)}, u32[]{:S(2)}, u32[]{:S(2)}) collective-permute-start(bf16[512,1280]{1,0:T(8,128)(2,1)S(1)} %multiply_convert_fusion.refs_6_.refs_4_.refs_2_.refs_5_), channel_id=1, source_target_pairs={{0,8},{8,0},{1,9},{9,1},{2,10},{10,2},{3,11},{11,3},{4,12},{12,4},... | collective-permute-start | bytes 3932168 | tf_op jit(solution)/shard_map/ppermute | solution.py:27
  67.4 17.9 %collective-permute-start.19 = (bf16[512,1280]{1,0:T(8,128)(2,1)}, bf16[512,1280]{1,0:T(8,128)(2,1)}, u32[]{:S(2)}, u32[]{:S(2)}) collective-permute-start(bf16[512,1280]{1,0:T(8,128)(2,1)} %collective-permute-done.1.refs_7_.refs_5_.refs_3_.refs_6_), channel_id=1, source_target_pairs={{0,8},{8,0},{1,9},{9,1},{2,10},{10,2},{3,11},{11,3},{4,12},{12,4},... | collective-permute-start | bytes 3932168 | tf_op jit(solution)/shard_map/ppermute | solution.py:27
  79.4 21.9 %collective-permute-start.12 = (bf16[512,1024]{1,0:T(8,128)(2,1)}, bf16[512,1024]{1,0:T(8,128)(2,1)}, u32[]{:S(2)}, u32[]{:S(2)}) collective-permute-start(bf16[512,1024]{1,0:T(8,128)(2,1)} %slice.44), channel_id=1, source_target_pairs={{0,1},{1,0},{2,3},{3,2},{4,5},{5,4},{6,7},{7,6},{8,9},{9,8},{10,11... | collective-permute-start | bytes 3145736 | tf_op jit(solution)/shard_map/ppermute | solution.py:27
  81.8 33.7 %collective-permute-start.10 = (bf16[768,1024]{1,0:T(8,128)(2,1)S(1)}, bf16[768,1024]{1,0:T(8,128)(2,1)S(1)}, u32[]{:S(2)}, u32[]{:S(2)}) collective-permute-start(bf16[768,1024]{1,0:T(8,128)(2,1)S(1)} %slice.43), channel_id=1, source_target_pairs={{0,2},{2,4},{4,6},{6,0},{8,14},{10,8},{12,10},{14,12},{1,3},{3,5},... | collective-permute-start | bytes 4718600 | tf_op jit(solution)/shard_map/ppermute | solution.py:23
  83.2 31.7 %collective-permute-start.13 = (bf16[512,1280]{1,0:T(8,128)(2,1)}, bf16[512,1280]{1,0:T(8,128)(2,1)}, u32[]{:S(2)}, u32[]{:S(2)}) collective-permute-start(bf16[512,1280]{1,0:T(8,128)(2,1)} %collective-permute-done.3.refs_14_.refs_12_.refs_10_.refs_13_), channel_id=1, source_target_pairs={{0,48},{16,0},{32,16},{48,32},{8,24},{24,40},{40,56},{56,8},{1,49}... | collective-permute-start | bytes 3932168 | tf_op jit(solution)/shard_map/ppermute | solution.py:23
  83.7 31.7 %collective-permute-start.14 = (bf16[512,1280]{1,0:T(8,128)(2,1)}, bf16[512,1280]{1,0:T(8,128)(2,1)}, u32[]{:S(2)}, u32[]{:S(2)}) collective-permute-start(bf16[512,1280]{1,0:T(8,128)(2,1)} %collective-permute-done.8.refs_15_.refs_13_.refs_11_.refs_14_), channel_id=1, source_target_pairs={{0,16},{16,32},{32,48},{48,0},{8,56},{24,8},{40,24},{56,40},{1,17}... | collective-permute-start | bytes 3932168 | tf_op jit(solution)/shard_map/ppermute | solution.py:23
  85.3 29.6 %collective-permute-start.11 = (bf16[512,1024]{1,0:T(8,128)(2,1)}, bf16[512,1024]{1,0:T(8,128)(2,1)}, u32[]{:S(2)}, u32[]{:S(2)}) collective-permute-start(bf16[512,1024]{1,0:T(8,128)(2,1)} %collective-permute-done.6.refs_4_), channel_id=1, source_target_pairs={{0,2},{2,4},{4,6},{6,0},{8,14},{10,8},{12,10},{14,12},{1,3},{3,5},... | collective-permute-start | bytes 3145736 | tf_op jit(solution)/shard_map/ppermute | solution.py:23
  101.3 16.9 %collective-permute-start.21 = (bf16[512,1280]{1,0:T(8,128)(2,1)S(1)}, bf16[512,1280]{1,0:T(8,128)(2,1)}, u32[]{:S(2)}, u32[]{:S(2)}) collective-permute-start(bf16[512,1280]{1,0:T(8,128)(2,1)S(1)} %copy-done.3), channel_id=1, source_target_pairs={{0,8},{8,0},{1,9},{9,1},{2,10},{10,2},{3,11},{11,3},{4,12},{12,4},... | collective-permute-start | bytes 3932168 | tf_op jit(solution)/shard_map/ppermute | solution.py:27
  124.4 25.9 %collective-permute-start.17 = (bf16[512,1024]{1,0:T(8,128)(2,1)}, bf16[512,1024]{1,0:T(8,128)(2,1)}, u32[]{:S(2)}, u32[]{:S(2)}) collective-permute-start(bf16[512,1024]{1,0:T(8,128)(2,1)} %pad_maximum_fusion), channel_id=1, source_target_pairs={{0,1},{1,0},{2,3},{3,2},{4,5},{5,4},{6,7},{7,6},{8,9},{9,8},{10,11... | collective-permute-start | bytes 3145736 | tf_op jit(solution)/shard_map/ppermute | solution.py:27
  125.7 26.9 %collective-permute-start.15 = (bf16[512,1024]{1,0:T(8,128)(2,1)}, bf16[512,1024]{1,0:T(8,128)(2,1)}, u32[]{:S(2)}, u32[]{:S(2)}) collective-permute-start(bf16[512,1024]{1,0:T(8,128)(2,1)} %collective-permute-done.11.refs_5_), channel_id=1, source_target_pairs={{0,2},{2,4},{4,6},{6,0},{8,14},{10,8},{12,10},{14,12},{1,3},{3,5},... | collective-permute-start | bytes 3145736 | tf_op jit(solution)/shard_map/ppermute | solution.py:23
  125.8 26.8 %collective-permute-start.16 = (bf16[512,1024]{1,0:T(8,128)(2,1)}, bf16[512,1024]{1,0:T(8,128)(2,1)}, u32[]{:S(2)}, u32[]{:S(2)}) collective-permute-start(bf16[512,1024]{1,0:T(8,128)(2,1)} %collective-permute-done.6.refs_4_), channel_id=1, source_target_pairs={{0,6},{2,0},{4,2},{6,4},{8,10},{10,12},{12,14},{14,8},{1,7},{3,1},... | collective-permute-start | bytes 3145736 | tf_op jit(solution)/shard_map/ppermute | solution.py:23
  153.7 27.2 %collective-permute-start.27 = (bf16[256,1024]{1,0:T(8,128)(2,1)S(1)}, bf16[256,1024]{1,0:T(8,128)(2,1)}, u32[]{:S(2)}, u32[]{:S(2)}) collective-permute-start(bf16[256,1024]{1,0:T(8,128)(2,1)S(1)} %slice.48), channel_id=1, source_target_pairs={{0,2},{2,4},{4,6},{6,0},{8,14},{10,8},{12,10},{14,12},{1,3},{3,5},... | collective-permute-start | bytes 1572872 | tf_op jit(solution)/shard_map/ppermute | solution.py:23
  153.8 27.1 %collective-permute-start.28 = (bf16[256,1024]{1,0:T(8,128)(2,1)S(1)}, bf16[256,1024]{1,0:T(8,128)(2,1)S(1)}, u32[]{:S(2)}, u32[]{:S(2)}) collective-permute-start(bf16[256,1024]{1,0:T(8,128)(2,1)S(1)} %slice.48), channel_id=1, source_target_pairs={{0,6},{2,0},{4,2},{6,4},{8,10},{10,12},{12,14},{14,8},{1,7},{3,1},... | collective-permute-start | bytes 1572872 | tf_op jit(solution)/shard_map/ppermute | solution.py:23
  158.1 22.0 %collective-permute-start.26 = (bf16[256,1024]{1,0:T(8,128)(2,1)S(1)}, bf16[256,1024]{1,0:T(8,128)(2,1)S(1)}, u32[]{:S(2)}, u32[]{:S(2)}) collective-permute-start(bf16[256,1024]{1,0:T(8,128)(2,1)S(1)} %slice.47), channel_id=1, source_target_pairs={{0,2},{2,4},{4,6},{6,0},{8,14},{10,8},{12,10},{14,12},{1,3},{3,5},... | collective-permute-start | bytes 1572872 | tf_op jit(solution)/shard_map/ppermute | solution.py:23
  158.2 23.5 %collective-permute-start.29 = (bf16[256,1024]{1,0:T(8,128)(2,1)S(1)}, bf16[256,1024]{1,0:T(8,128)(2,1)S(1)}, u32[]{:S(2)}, u32[]{:S(2)}) collective-permute-start(bf16[256,1024]{1,0:T(8,128)(2,1)S(1)} %slice.49), channel_id=1, source_target_pairs={{0,1},{1,0},{2,3},{3,2},{4,5},{5,4},{6,7},{7,6},{8,9},{9,8},{10,11... | collective-permute-start | bytes 1572872 | tf_op jit(solution)/shard_map/ppermute | solution.py:27
  181.7 12.2 %collective-permute-start.31 = (bf16[256,1024]{1,0:T(8,128)(2,1)}, bf16[256,1024]{1,0:T(8,128)(2,1)}, u32[]{:S(2)}, u32[]{:S(2)}) collective-permute-start(bf16[256,1024]{1,0:T(8,128)(2,1)} %collective-permute-done.27.refs_3_), channel_id=1, source_target_pairs={{0,2},{2,4},{4,6},{6,0},{8,14},{10,8},{12,10},{14,12},{1,3},{3,5},... | collective-permute-start | bytes 1572872 | tf_op jit(solution)/shard_map/ppermute | solution.py:23
  (32 other events, 461.1 us)

commit v2 on v1

--- a/solution.py
+++ b/solution.py
@@ -27,9 +27,9 @@
     return lax.ppermute(a, axis, [(0, 1), (1, 0)])
 
 
-def flip(a, axis, bit):
-    size = 4 if axis == "y" else 2
-    return lax.ppermute(a, axis, [(i, i ^ bit) for i in range(size)])
+def squares(a):
+    wide = a.astype(jnp.float32)
+    return jnp.sum(wide * wide, axis=-1)
 
 
 def together(*arrays):
@@ -75,8 +75,13 @@
     n = len(parts)
     rows = sum(count for _, _, count in where[0])
     feats = flat[0].shape[1]
-    deep, width = weights[0].shape
-    extra = [] if acc_in is None else [acc_in]
+    deep, width = weights[0][0].shape[0], weights[0][0].shape[1]
+    stores = []
+    for array, _ in weights:
+        if not any(have is array for have in stores):
+            stores.append(array)
+    spots_w = [(next(i for i, have in enumerate(stores) if have is array), row) for array, row in weights]
+    extra = [] if acc_in is None else [acc_in[0]]
     if final is not None:
         inv, length, out_row, out_old = final
         extra += [inv, length] + ([] if out_old is None else [out_old])
@@ -84,7 +89,7 @@
     def body(sel_ref, *refs):
         refs = list(refs)
         pieces = [refs.pop(0) for _ in flat]
-        blocks = [refs.pop(0) for _ in weights]
+        blocks = [refs.pop(0) for _ in stores]
         acc_ref = None if acc_in is None else refs.pop(0)
         if final is not None:
             inv_ref, length_ref = refs.pop(0), refs.pop(0)
@@ -104,16 +109,16 @@
                         ).start()
                         to += count
             for side in range(2):
-                for j, block in enumerate(blocks):
+                for j, (i, row) in enumerate(spots_w):
                     @pl.when(sel_ref[2 * k + side] == j)
-                    def _(block=block, side=side):
+                    def _(i=i, row=row, side=side):
                         pltpu.make_async_copy(
-                            block, w_buf.at[slot, pl.ds(side * deep, deep)], sem_w.at[slot]
+                            blocks[i].at[pl.ds(row, deep)], w_buf.at[slot, pl.ds(side * deep, deep)], sem_w.at[slot]
                         ).start()
 
         fetch(0, 0)
         if acc_ref is not None:
-            load = pltpu.make_async_copy(acc_ref, acc, sem_c)
+            load = pltpu.make_async_copy(acc_ref.at[pl.ds(acc_in[1], rows)], acc, sem_c)
             load.start()
             load.wait()
         else:
@@ -143,9 +148,9 @@
         save.start()
         save.wait()
 
-    anywhere = pl.BlockSpec(memory_space=pl.ANY)
+    anywhere, main = pl.BlockSpec(memory_space=pl.ANY), pl.BlockSpec(memory_space=pl.ANY)
     smem = pl.BlockSpec(memory_space=pltpu.SMEM)
-    specs = [smem] + [anywhere] * (len(flat) + len(weights) + (acc_in is not None))
+    specs = [smem] + [anywhere] * (len(flat) + len(stores)) + [main] * (acc_in is not None)
     scratch = [
         pltpu.VMEM((2, rows, feats), jnp.bfloat16),
         pltpu.VMEM((2, 2 * deep, width), jnp.bfloat16),
@@ -165,17 +170,17 @@
         flops += 6 * 10**9
         if out_old is not None:
             aliases[len(specs)] = 0
-            specs.append(anywhere)
+            specs.append(main)
     return pl.pallas_call(
         body,
         in_specs=specs,
-        out_specs=anywhere,
+        out_specs=main,
         out_shape=out,
         scratch_shapes=scratch,
         input_output_aliases=aliases,
-        compiler_params=pltpu.CompilerParams(vmem_limit_bytes=30 << 20),
+        compiler_params=pltpu.CompilerParams(vmem_limit_bytes=56 << 20),
         cost_estimate=pl.CostEstimate(flops=flops, bytes_accessed=n * 4 * 10**6, transcendentals=0),
-    )(sel, *flat, *weights, *extra)
+    )(sel, *flat, *stores, *extra)
 
 
 def local(hidden, norm_gain, lengths, query_weight, keyval_weight):
@@ -190,34 +195,46 @@
     own = (own.astype(jnp.float32) * gain[:, None]).astype(jnp.bfloat16)
     width = own.shape[1]
 
-    wide = hidden.astype(jnp.float32)
-    square = jnp.sum(wide * wide, axis=-1).reshape(8, -1)
-    square = square + flip(square, "y", 1)
-
-    h0 = hidden
-    far = swap(own, "zh")
+    half = span // 2
+    h0, w0 = hidden, own
+    f0 = swap(w0, "zh")
+    w1, w3 = ring(w0, "x"), ring(w0, "x", -1)
     h1 = ring(h0, "y")
-    w1, w3 = ring(own, "x"), ring(own, "x", -1)
-    v0 = swap(own, "c")
-    h0, w0, h1, w1, w3, f0, square = together(h0, own, h1, w1, w3, far, square)
-    square = square + flip(square, "y", 2)
-    h3 = ring(h0, "y", -1)
-    lo0 = swap(h0[:span], "zl")
+    h_lo, h_hi = h0[:span], h0[span:]
+    h3_lo = ring(h_lo, "y", -1)
+    square = squares(h0)
+    f0, w0, w1, w3, h0, h1, h3_lo, h_lo, h_hi, square = together(f0, w0, w1, w3, h0, h1, h3_lo, h_lo, h_hi, square)
     w2, f1 = ring(w1, "x"), ring(f0, "x")
-    v1, v3 = swap(w1, "c"), swap(w3, "c")
-    h0, h1, h3, lo0, w2, f0, f1, square = together(h0, h1, h3, lo0, w2, f0, f1, square)
-    square = square + flip(square, "zl", 1)
-    h2a = ring(h1[:cut], "y")
+    h3_hi = ring(h_hi, "y", -1)
+    h2_lo = ring(h1[:span], "y")
+    lo0 = swap(h_lo, "zl")
+    others = jnp.concatenate([w0, w1, w3], axis=0)
+    square += squares(h1)
+    h1_hi = h1[span:]
+    w2, f0, f1, h0, h1, h1_hi, h2_lo, h3_hi, lo0, h_hi, square, others = together(
+        w2, f0, f1, h0, h1, h1_hi, h2_lo, h3_hi, lo0, h_hi, square, others
+    )
+    others = swap(others, "c")
+    f3, f2 = ring(f0, "x", -1), ring(f1, "x")
+    h2_hi = ring(h1_hi, "y")
+    hi0 = swap(h_hi, "zl")
     lo1 = ring(lo0, "y")
-    hi0 = swap(h0[span:], "zl")
-    f3, f2 = ring(f0, "x", -1), ring(f1, "x")
-    v2, g0, g1 = swap(w2, "c"), swap(f0, "c"), swap(f1, "c")
-    h1, h3, h2a, lo0, lo1, hi0, f3, f2 = together(h1, h3, h2a, lo0, lo1, hi0, f3, f2)
-    g3, g2 = swap(f3, "c"), swap(f2, "c")
+    more = jnp.concatenate([w2, f0, f1], axis=0)
+    square += jnp.concatenate([squares(h2_lo) + squares(h3_lo), squares(h3_hi)], axis=0)
+    tail = jnp.concatenate([h1_hi[:half], h3_hi[:half]], axis=0)
+    f3, f2, h2_lo, h2_hi, h3_hi, hi0, lo0, lo1, tail, square, others, more = together(
+        f3, f2, h2_lo, h2_hi, h3_hi, hi0, lo0, lo1, tail, square, others, more
+    )
+    more = swap(more, "c")
+    last = swap(jnp.concatenate([f2, f3], axis=0), "c")
     lo2, lo3 = ring(lo1, "y"), ring(lo0, "y", -1)
-    tails = swap(jnp.concatenate([h1[span:cut], h3[span:cut]], axis=0), "zl")
-    weights = [w0, w1, w2, w3, v0, v1, v2, v3, f0, f1, f2, f3, g0, g1, g2, g3]
-    half = span // 2
+    mid0 = hi0[half:]
+    mid1 = ring(mid0, "y")
+    tails = swap(tail, "zl")
+    square += jnp.concatenate([jnp.zeros_like(square[:span]), squares(h2_hi)], axis=0)
+    square = square.reshape(8, -1)
+    weights = [(w0, 0), (w1, 0), (w2, 0), (w3, 0), (others, 0), (others, rows), (more, 0), (others, 2 * rows)]
+    weights += [(f0, 0), (f1, 0), (f2, 0), (f3, 0), (more, rows), (more, 2 * rows), (last, 0), (last, rows)]
 
     def choose(*ones):
         step = jnp.array([k for k, _ in ones], jnp.int32)
@@ -228,25 +245,20 @@
         k = jnp.where(core == 0, x - x_at[:, None], x_at[:, None] - x) & 3
         return (((z_at ^ zh)[:, None]) * 8 + (core ^ c) * 4 + k).reshape(-1)
 
-    first = [(h0, 0, span)], [(h1, 0, span)], [(h2a, 0, span)], [(h3, 0, span)], [(lo0, 0, span)], [(lo1, 0, span)]
-    acc0 = stage(first, choose((0, 0), (1, 0), (2, 0), (3, 0), (0, 1), (1, 1)), weights)
-    lo2, lo3, tails, h1, h2a, hi0, acc0 = together(lo2, lo3, tails, h1, h2a, hi0, acc0)
-    h2b = ring(h1[cut:], "y")
-    mid0 = hi0[half:]
-    mid1, mid3 = ring(mid0, "y"), ring(mid0, "y", -1)
-    tail2 = swap(h2a[span:], "zl")
+    parts = [(h0, 0, 2 * span)], [(h1, 0, 2 * span)], [(h2_lo, 0, span), (h2_hi, 0, span)], [(h3_lo, 0, span), (h3_hi, 0, span)]
+    parts += ([(lo0, 0, span), (hi0, 0, span)],)
+    acc = stage(parts, choose((0, 0), (1, 0), (2, 0), (3, 0), (0, 1)), weights)
+    tail = h2_hi[:half]
+    lo2, lo3, mid0, mid1, tails, tail, acc, square = together(lo2, lo3, mid0, mid1, tails, tail, acc, square)
+    square = square + swap(square, "zl")
+    mid2, mid3 = ring(mid1, "y"), ring(mid0, "y", -1)
+    tail2 = swap(tail, "zl")
     inv = lax.rsqrt(square.reshape(-1, 1) / (feats * 8) + EPS)
-    out = stage(
-        ([(lo2, 0, span)], [(lo3, 0, span)]), choose((2, 1), (3, 1)), weights, acc0, (inv[:span], lengths[:1], 0, None)
-    )
-    parts = [(h0, span, span)], [(h1, span, span)], [(h3, span, span)], [(hi0, 0, span)]
-    acc1 = stage(parts, choose((0, 0), (1, 0), (3, 0), (0, 1)), weights)
-    h2b, mid1, mid3, tail2, acc1, out = together(h2b, mid1, mid3, tail2, acc1, out)
-    mid2 = ring(mid1, "y")
-    parts = [(h2a, span, half), (h2b, 0, half)], [(tails, 0, half), (mid1, 0, half)], [(tails, half, half), (mid3, 0, half)]
-    acc1 = stage(parts, choose((2, 0), (1, 1), (3, 1)), weights, acc1)
-    parts = ([(tail2, 0, half), (mid2, 0, half)],)
-    return stage(parts, choose((2, 1)), weights, acc1, (inv[span:], lengths[1:], span, out))
+    parts = [(lo1, 0, span)], [(lo2, 0, span)], [(lo3, 0, span)]
+    out = stage(parts, choose((1, 1), (2, 1), (3, 1)), weights, (acc, 0), (inv[:span], lengths[:1], 0, None))
+    mid2, mid3, tail2, out = together(mid2, mid3, tail2, out)
+    parts = [(tails, 0, half), (mid1, 0, half)], [(tails, half, half), (mid3, 0, half)], [(tail2, 0, half), (mid2, 0, half)]
+    return stage(parts, choose((1, 1), (3, 1), (2, 1)), weights, (acc, span), (inv[span:], lengths[1:], span, out))
 
 
 def solution(mesh):

time: 207 us -> 180 us (0.87)
  starting transfers between devices: 44.5 us -> 34.4 us
  waiting for transfers between devices: 82.6 us -> 74.5 us
  Pallas kernels: 53.6 us -> 46 us
  other arithmetic: 3.48 us -> 10.3 us
  local copies, waits for them, and re-layouts: 19.8 us -> 13.9 us
    ppermute x16 -> x17, waiting for transfers between devices: 38.4 us -> 64.5 us  [ring(): return lax.ppermute(a, ('c', 'y') if axis == 'y' else ('x', 'c'), perm)]
    ppermute x3 -> x0, waiting for transfers between devices: 17.3 us -> none  [flip(): return lax.ppermute(a, axis, [(i, i ^ bit) for i in range(size)])]
    ppermute x13 -> x9, waiting for transfers between devices: 27 us -> 10 us  [swap(): return lax.ppermute(a, axis, [(0, 1), (1, 0)])]
    ppermute x13 -> x9, starting transfers between devices: 23.4 us -> 9.54 us  [swap(): return lax.ppermute(a, axis, [(0, 1), (1, 0)])]
    pallas_call x5 -> x3, Pallas kernels: 53.6 us -> 46 us  [stage(): pl.pallas_call(body, in_specs=specs, out_specs=main, out_shape=out, scrat...]
    ppermute x16 -> x17, starting transfers between devices: 17.8 us -> 24.8 us  [ring(): return lax.ppermute(a, ('c', 'y') if axis == 'y' else ('x', 'c'), perm)]
    unnamed x49 -> x63, local copies, waits for them, and re-layouts: 10.5 us -> 3.93 us
    reduce_sum x1 -> x5, other arithmetic: 0.48 us -> 4.81 us  [squares(): return jnp.sum(wide * wide, axis=-1)]
  transfers between devices with their start and end apart: 32 -> 26, of which waited for: 12 -> 12; matrix products, arithmetic and copies ran while one was open for 7% -> 12% of each run, Pallas kernels for 22% -> 18%
where the time goes in v2:
time: 180 us
  waiting for transfers between devices  74.5 us (41%)
  Pallas kernels  46 us (26%)
  starting transfers between devices  34.4 us (19%)
  local copies, waits for them, and re-layouts  13.9 us (8%)
  other arithmetic  10.3 us (6%)
    ppermute x17, waiting for transfers between devices, ring(): return lax.ppermute(a, ('c', 'y') if axis == 'y' else ('x', 'c'), perm)  64.5 us
    pallas_call x3, Pallas kernels, stage(): pl.pallas_call(body, in_specs=specs, out_specs=main, out_shape=out, scrat...  46 us
    ppermute x17, starting transfers between devices, ring(): return lax.ppermute(a, ('c', 'y') if axis == 'y' else ('x', 'c'), perm)  24.8 us
    ppermute x9, waiting for transfers between devices, swap(): return lax.ppermute(a, axis, [(0, 1), (1, 0)])  10 us
    ppermute x9, starting transfers between devices, swap(): return lax.ppermute(a, axis, [(0, 1), (1, 0)])  9.54 us
    reduce_sum x5, other arithmetic, squares(): return jnp.sum(wide * wide, axis=-1)  4.81 us
    unnamed x63, local copies, waits for them, and re-layouts  3.93 us
  transfers between devices with their start and end apart: 26, of which 12 were waited for; matrix products, arithmetic and copies ran while one was open for 12% of the time, Pallas kernels for 18%

profile of v2, /device:TPU:0, one launch (start us, length us, event | category | flops | bytes accessed | tf_op | source)
XLA Modules:
  0.0 179.6 jit_solution(9128521538772244535)
XLA Ops:
  4.9 4.0 %collective-permute-start = (bf16[512,1280]{1,0:T(8,128)(2,1)S(1)}, bf16[512,1280]{1,0:T(8,128)(2,1)S(1)}, u32[]{:S(2)}, u32[]{:S(2)}) collective-permute-start(bf16[512,1280]{1,0:T(8,128)(2,1)S(1)} %multiply_convert_fusion.refs_8_.refs_3_.refs_5_), channel_id=1, source_target_pairs={{0,64},{64,0},{1,65},{65,1},{2,66},{66,2},{3,67},{67,3},{4,68},{68... | collective-permute-start | bytes 3932168 | tf_op jit(solution)/shard_map/ppermute | solution.py:27
  10.4 1.7 collective-permute-start.2
  12.3 1.8 %collective-permute-start.4 = (bf16[512,1024]{1,0:T(8,128)(2,1)S(1)}, bf16[512,1024]{1,0:T(8,128)(2,1)S(1)}, u32[]{:S(2)}, u32[]{:S(2)}) collective-permute-start(bf16[512,1024]{1,0:T(8,128)(2,1)S(1)} %get-tuple-element.56), channel_id=1, source_target_pairs={{0,6},{2,0},{4,2},{6,4},{8,10},{10,12},{12,14},{14,8},{1,7},{3,1},... | collective-permute-start | bytes 3145736 | tf_op jit(solution)/shard_map/ppermute | solution.py:23
  14.6 22.3 %collective-permute-done.4.refs_4_ = bf16[512,1024]{1,0:T(8,128)(2,1)S(1)} collective-permute-done((bf16[512,1024]{1,0:T(8,128)(2,1)S(1)}, bf16[512,1024]{1,0:T(8,128)(2,1)S(1)}, u32[]{:S(2)}, u32[]{:S(2)}) %collective-permute-start.4) | collective-permute-done | bytes 1048608 | tf_op jit(solution)/shard_map/ppermute | solution.py:23
  41.8 1.8 %collective-permute-start.6 = (bf16[512,1280]{1,0:T(8,128)(2,1)S(1)}, bf16[512,1280]{1,0:T(8,128)(2,1)S(1)}, u32[]{:S(2)}, u32[]{:S(2)}) collective-permute-start(bf16[512,1280]{1,0:T(8,128)(2,1)S(1)} %collective-permute-done.refs_14_.refs_9_.refs_11_), channel_id=1, source_target_pairs={{0,16},{16,32},{32,48},{48,0},{8,56},{24,8},{40,24},{56,40},{1,17}... | collective-permute-start | bytes 3932168 | tf_op jit(solution)/shard_map/ppermute | solution.py:23
  43.6 1.7 fusion.13
  45.8 2.8 %collective-permute-start.8 = (bf16[512,1024]{1,0:T(8,128)(2,1)S(1)}, bf16[512,1024]{1,0:T(8,128)(2,1)S(1)}, u32[]{:S(2)}, u32[]{:S(2)}) collective-permute-start(bf16[512,1024]{1,0:T(8,128)(2,1)S(1)} %get-tuple-element.65), channel_id=1, source_target_pairs={{0,6},{2,0},{4,2},{6,4},{8,10},{10,12},{12,14},{14,8},{1,7},{3,1},... | collective-permute-start | bytes 3145736 | tf_op jit(solution)/shard_map/ppermute | solution.py:23
  49.7 2.1 %multiply_reduce_fusion = f32[1024]{0:T(1024)S(1)} fusion(bf16[1024,1024]{1,0:T(8,128)(2,1)} %collective-permute-done.3.refs_1_), kind=kLoop, calls=%fused_computation | loop fusion | flops 3144704 | bytes 2101248 | tf_op jit(solution)/shard_map/reduce_sum | solution.py:32
  52.2 19.7 %collective-permute-done.7.refs_2_ = bf16[512,1024]{1,0:T(8,128)(2,1)S(1)} collective-permute-done((bf16[512,1024]{1,0:T(8,128)(2,1)S(1)}, bf16[512,1024]{1,0:T(8,128)(2,1)S(1)}, u32[]{:S(2)}, u32[]{:S(2)}) %collective-permute-start.7) | collective-permute-done | bytes 1048608 | tf_op jit(solution)/shard_map/ppermute | solution.py:23
  72.0 1.9 %collective-permute-done.6.refs_15_.refs_10_.refs_12_ = bf16[512,1280]{1,0:T(8,128)(2,1)S(1)} collective-permute-done((bf16[512,1280]{1,0:T(8,128)(2,1)S(1)}, bf16[512,1280]{1,0:T(8,128)(2,1)S(1)}, u32[]{:S(2)}, u32[]{:S(2)}) %collective-permute-start.6) | collective-permute-done | bytes 1310752 | tf_op jit(solution)/shard_map/ppermute | solution.py:23
  73.9 2.2 %collective-permute-start.12 = (bf16[512,1024]{1,0:T(8,128)(2,1)S(1)}, bf16[512,1024]{1,0:T(8,128)(2,1)}, u32[]{:S(2)}, u32[]{:S(2)}) collective-permute-start(bf16[512,1024]{1,0:T(8,128)(2,1)S(1)} %get-tuple-element.63), channel_id=1, source_target_pairs={{0,2},{2,4},{4,6},{6,0},{8,14},{10,8},{12,10},{14,12},{1,3},{3,5},... | collective-permute-start | bytes 3145736 | tf_op jit(solution)/shard_map/ppermute | solution.py:23
  76.1 2.0 %collective-permute-start.11 = (bf16[512,1280]{1,0:T(8,128)(2,1)S(1)}, bf16[512,1280]{1,0:T(8,128)(2,1)S(1)}, u32[]{:S(2)}, u32[]{:S(2)}) collective-permute-start(bf16[512,1280]{1,0:T(8,128)(2,1)S(1)} %collective-permute-done.6.refs_15_.refs_10_.refs_12_), channel_id=1, source_target_pairs={{0,16},{16,32},{32,48},{48,0},{8,56},{24,8},{40,24},{56,40},{1,17}... | collective-permute-start | bytes 3932168 | tf_op jit(solution)/shard_map/ppermute | solution.py:23
  79.5 10.6 %collective-permute-done.12.refs_3_ = bf16[512,1024]{1,0:T(8,128)(2,1)} collective-permute-done((bf16[512,1024]{1,0:T(8,128)(2,1)S(1)}, bf16[512,1024]{1,0:T(8,128)(2,1)}, u32[]{:S(2)}, u32[]{:S(2)}) %collective-permute-start.12) | collective-permute-done | bytes 1048608 | tf_op jit(solution)/shard_map/ppermute | solution.py:23
  92.6 2.1 %pad_maximum_fusion.1 = bf16[1536,1280]{1,0:T(8,128)(2,1)} fusion(bf16[512,1280]{1,0:T(8,128)(2,1)S(1)} %collective-permute-done.6.refs_15_.refs_10_.refs_12_, bf16[512,1280]{1,0:T(8,128)(2,1)S(1)} %collective-permute-done.refs_14_.refs_9_.refs_11_, bf16[512,1280]{1,0:T(8,128)(2,1)S(1)} %collective-permute-done.5.refs_10_.refs_5_.refs_7_), kind=kLoop, calls=%fused_computation.3 | loop fusion | flops 11796480 | bytes 7864320 | tf_op jit(solution)/shard_map/concatenate | solution.py:222
  94.8 8.6 %collective-permute-done.13.refs_7_ = bf16[512,1024]{1,0:T(8,128)(2,1)S(1)} collective-permute-done((bf16[512,1024]{1,0:T(8,128)(2,1)S(1)}, bf16[512,1024]{1,0:T(8,128)(2,1)S(1)}, u32[]{:S(2)}, u32[]{:S(2)}) %collective-permute-start.13) | collective-permute-done | bytes 1048608 | tf_op jit(solution)/shard_map/ppermute | solution.py:27
  103.4 2.6 %collective-permute-done.14.refs_0_ = bf16[512,1024]{1,0:T(8,128)(2,1)S(1)} collective-permute-done((bf16[512,1024]{1,0:T(8,128)(2,1)S(1)}, bf16[512,1024]{1,0:T(8,128)(2,1)S(1)}, u32[]{:S(2)}, u32[]{:S(2)}) %collective-permute-start.14) | collective-permute-done | bytes 1048608 | tf_op jit(solution)/shard_map/ppermute | solution.py:23
  107.3 1.9 %copy-done.23 = bf16[1536,1280]{1,0:T(8,128)(2,1)} copy-done((bf16[1536,1280]{1,0:T(8,128)(2,1)}, bf16[1536,1280]{1,0:T(8,128)(2,1)S(1)}, u32[]{:S(2)}) %copy-start.23) | copy-done | bytes 3932184
  111.8 2.0 %collective-permute-start.17 = (bf16[512,1024]{1,0:T(8,128)(2,1)}, bf16[512,1024]{1,0:T(8,128)(2,1)S(1)}, u32[]{:S(2)}, u32[]{:S(2)}) collective-permute-start(bf16[512,1024]{1,0:T(8,128)(2,1)} %copy-done.24), channel_id=1, source_target_pairs={{0,6},{2,0},{4,2},{6,4},{8,10},{10,12},{12,14},{14,8},{1,7},{3,1},... | collective-permute-start | bytes 3145736 | tf_op jit(solution)/shard_map/ppermute | solution.py:23
  115.0 1.9 %slice.49 = bf16[256,1024]{1,0:T(8,128)(2,1)} slice(bf16[512,1024]{1,0:T(8,128)(2,1)} %collective-permute-done.12.refs_3_), slice={[0:256], [0:1024]} | slice | bytes 1048576 | tf_op jit(solution)/shard_map/slice | solution.py:251
  119.7 20.0 %shard_map.136.refs_14_.refs_16_ = f32[1024,1280]{1,0:T(8,128)} custom-call(s32[10]{0:T(128)} %add.147.sel_ref, bf16[1024,1024]{1,0:T(8,128)(2,1)} %refs_0_, bf16[1024,1024]{1,0:T(8,128)(2,1)} %collective-permute-done.3.refs_1_, bf16[512,1024]{1,0:T(8,128)(2,1)} %copy-done.11, bf16[512,1024]{1,0:T(8,128)(2,1)} %collective-permute-done.12.refs_3_, ...), custom_call_target="tpu_custom_call" | custom-call | flops 13421772800 | bytes 20000000 | tf_op jit(solution)/shard_map/pallas_call | solution.py:174
  139.7 3.9 %collective-permute-done.18.refs_1_ = bf16[256,1024]{1,0:T(8,128)(2,1)S(1)} collective-permute-done((bf16[256,1024]{1,0:T(8,128)(2,1)S(1)}, bf16[256,1024]{1,0:T(8,128)(2,1)S(1)}, u32[]{:S(2)}, u32[]{:S(2)}) %collective-permute-start.18) | collective-permute-done | bytes 524320 | tf_op jit(solution)/shard_map/ppermute | solution.py:23
  146.6 1.7 collective-permute-start.22
  152.6 13.1 %shard_map.137.refs_19_ = bf16[1024,1024]{1,0:T(8,128)(2,1)} custom-call(s32[6]{0:T(128)} %add.155.sel_ref, bf16[512,1024]{1,0:T(8,128)(2,1)} %copy-done.25, bf16[512,1024]{1,0:T(8,128)(2,1)} %copy-done.27, bf16[512,1024]{1,0:T(8,128)(2,1)} %copy-done.28, bf16[512,1280]{1,0:T(8,128)(2,1)} %copy-done.1, bf16[512,1280]{1,0:T(8,128)(2,1)} %copy-done.6, ...), custom_call_target="tpu_custom_call" | custom-call | flops 10026531840 | bytes 12000000 | tf_op jit(solution)/shard_map/pallas_call | solution.py:174
  166.5 12.9 %shard_map.138 = bf16[1024,1024]{1,0:T(8,128)(2,1)} custom-call(s32[6]{0:T(128)} %add.134.sel_ref, bf16[512,1024]{1,0:T(8,128)(2,1)} %copy-done.26, bf16[256,1024]{1,0:T(8,128)(2,1)} %copy-done.29, bf16[256,1024]{1,0:T(8,128)(2,1)} %collective-permute-done.23.refs_2_, ...), custom_call_target="tpu_custom_call", output_to_operand_aliasing={{}: (20, {})} | custom-call | flops 10026531840 | bytes 12000000 | tf_op jit(solution)/shard_map/pallas_call | solution.py:174
  (132 shorter events, 33.8 us)
Async XLA Ops:
  0.0 40.6 %collective-permute-start.3 = (bf16[1024,1024]{1,0:T(8,128)(2,1)}, bf16[1024,1024]{1,0:T(8,128)(2,1)}, u32[]{:S(2)}, u32[]{:S(2)}) collective-permute-start(bf16[1024,1024]{1,0:T(8,128)(2,1)} %refs_0_), channel_id=1, source_target_pairs={{0,2},{2,4},{4,6},{6,0},{8,14},{10,8},{12,10},{14,12},{1,3},{3,5},... | collective-permute-start | bytes 6291464 | tf_op jit(solution)/shard_map/ppermute | solution.py:23
  4.9 33.3 %collective-permute-start = (bf16[512,1280]{1,0:T(8,128)(2,1)S(1)}, bf16[512,1280]{1,0:T(8,128)(2,1)S(1)}, u32[]{:S(2)}, u32[]{:S(2)}) collective-permute-start(bf16[512,1280]{1,0:T(8,128)(2,1)S(1)} %multiply_convert_fusion.refs_8_.refs_3_.refs_5_), channel_id=1, source_target_pairs={{0,64},{64,0},{1,65},{65,1},{2,66},{66,2},{3,67},{67,3},{4,68},{68... | collective-permute-start | bytes 3932168 | tf_op jit(solution)/shard_map/ppermute | solution.py:27
  8.9 30.6 %collective-permute-start.1 = (bf16[512,1280]{1,0:T(8,128)(2,1)S(1)}, bf16[512,1280]{1,0:T(8,128)(2,1)S(1)}, u32[]{:S(2)}, u32[]{:S(2)}) collective-permute-start(bf16[512,1280]{1,0:T(8,128)(2,1)S(1)} %multiply_convert_fusion.refs_8_.refs_3_.refs_5_), channel_id=1, source_target_pairs={{0,16},{16,32},{32,48},{48,0},{8,56},{24,8},{40,24},{56,40},{1,17}... | collective-permute-start | bytes 3932168 | tf_op jit(solution)/shard_map/ppermute | solution.py:23
  10.4 30.2 %collective-permute-start.2 = (bf16[512,1280]{1,0:T(8,128)(2,1)S(1)}, bf16[512,1280]{1,0:T(8,128)(2,1)S(1)}, u32[]{:S(2)}, u32[]{:S(2)}) collective-permute-start(bf16[512,1280]{1,0:T(8,128)(2,1)S(1)} %multiply_convert_fusion.refs_8_.refs_3_.refs_5_), channel_id=1, source_target_pairs={{0,48},{16,0},{32,16},{48,32},{8,24},{24,40},{40,56},{56,8},{1,49}... | collective-permute-start | bytes 3932168 | tf_op jit(solution)/shard_map/ppermute | solution.py:23
  12.3 24.7 %collective-permute-start.4 = (bf16[512,1024]{1,0:T(8,128)(2,1)S(1)}, bf16[512,1024]{1,0:T(8,128)(2,1)S(1)}, u32[]{:S(2)}, u32[]{:S(2)}) collective-permute-start(bf16[512,1024]{1,0:T(8,128)(2,1)S(1)} %get-tuple-element.56), channel_id=1, source_target_pairs={{0,6},{2,0},{4,2},{6,4},{8,10},{10,12},{12,14},{14,8},{1,7},{3,1},... | collective-permute-start | bytes 3145736 | tf_op jit(solution)/shard_map/ppermute | solution.py:23
  40.6 31.4 %collective-permute-start.5 = (bf16[512,1280]{1,0:T(8,128)(2,1)S(1)}, bf16[512,1280]{1,0:T(8,128)(2,1)S(1)}, u32[]{:S(2)}, u32[]{:S(2)}) collective-permute-start(bf16[512,1280]{1,0:T(8,128)(2,1)S(1)} %collective-permute-done.1.refs_9_.refs_4_.refs_6_), channel_id=1, source_target_pairs={{0,16},{16,32},{32,48},{48,0},{8,56},{24,8},{40,24},{56,40},{1,17}... | collective-permute-start | bytes 3932168 | tf_op jit(solution)/shard_map/ppermute | solution.py:23
  41.8 32.1 %collective-permute-start.6 = (bf16[512,1280]{1,0:T(8,128)(2,1)S(1)}, bf16[512,1280]{1,0:T(8,128)(2,1)S(1)}, u32[]{:S(2)}, u32[]{:S(2)}) collective-permute-start(bf16[512,1280]{1,0:T(8,128)(2,1)S(1)} %collective-permute-done.refs_14_.refs_9_.refs_11_), channel_id=1, source_target_pairs={{0,16},{16,32},{32,48},{48,0},{8,56},{24,8},{40,24},{56,40},{1,17}... | collective-permute-start | bytes 3932168 | tf_op jit(solution)/shard_map/ppermute | solution.py:23
  45.3 26.5 %collective-permute-start.7 = (bf16[512,1024]{1,0:T(8,128)(2,1)S(1)}, bf16[512,1024]{1,0:T(8,128)(2,1)S(1)}, u32[]{:S(2)}, u32[]{:S(2)}) collective-permute-start(bf16[512,1024]{1,0:T(8,128)(2,1)S(1)} %get-tuple-element.103), channel_id=1, source_target_pairs={{0,2},{2,4},{4,6},{6,0},{8,14},{10,8},{12,10},{14,12},{1,3},{3,5},... | collective-permute-start | bytes 3145736 | tf_op jit(solution)/shard_map/ppermute | solution.py:23
  45.8 26.0 %collective-permute-start.8 = (bf16[512,1024]{1,0:T(8,128)(2,1)S(1)}, bf16[512,1024]{1,0:T(8,128)(2,1)S(1)}, u32[]{:S(2)}, u32[]{:S(2)}) collective-permute-start(bf16[512,1024]{1,0:T(8,128)(2,1)S(1)} %get-tuple-element.65), channel_id=1, source_target_pairs={{0,6},{2,0},{4,2},{6,4},{8,10},{10,12},{12,14},{14,8},{1,7},{3,1},... | collective-permute-start | bytes 3145736 | tf_op jit(solution)/shard_map/ppermute | solution.py:23
  48.6 23.4 %collective-permute-start.9 = (bf16[512,1024]{1,0:T(8,128)(2,1)S(1)}, bf16[512,1024]{1,0:T(8,128)(2,1)S(1)}, u32[]{:S(2)}, u32[]{:S(2)}) collective-permute-start(bf16[512,1024]{1,0:T(8,128)(2,1)S(1)} %get-tuple-element.56), channel_id=1, source_target_pairs={{0,1},{1,0},{2,3},{3,2},{4,5},{5,4},{6,7},{7,6},{8,9},{9,8},{10,11... | collective-permute-start | bytes 3145736 | tf_op jit(solution)/shard_map/ppermute | solution.py:27
  73.9 33.3 %collective-permute-start.15 = (bf16[1536,1280]{1,0:T(8,128)(2,1)S(1)}, bf16[1536,1280]{1,0:T(8,128)(2,1)S(1)}, u32[]{:S(2)}, u32[]{:S(2)}) collective-permute-start(bf16[1536,1280]{1,0:T(8,128)(2,1)S(1)} %pad_maximum_fusion), channel_id=1, source_target_pairs={{0,8},{8,0},{1,9},{9,1},{2,10},{10,2},{3,11},{11,3},{4,12},{12,4},... | collective-permute-start | bytes 11796488 | tf_op jit(solution)/shard_map/ppermute | solution.py:27
  73.9 16.1 %collective-permute-start.12 = (bf16[512,1024]{1,0:T(8,128)(2,1)S(1)}, bf16[512,1024]{1,0:T(8,128)(2,1)}, u32[]{:S(2)}, u32[]{:S(2)}) collective-permute-start(bf16[512,1024]{1,0:T(8,128)(2,1)S(1)} %get-tuple-element.63), channel_id=1, source_target_pairs={{0,2},{2,4},{4,6},{6,0},{8,14},{10,8},{12,10},{14,12},{1,3},{3,5},... | collective-permute-start | bytes 3145736 | tf_op jit(solution)/shard_map/ppermute | solution.py:23
  76.1 30.0 %collective-permute-start.10 = (bf16[512,1280]{1,0:T(8,128)(2,1)S(1)}, bf16[512,1280]{1,0:T(8,128)(2,1)S(1)}, u32[]{:S(2)}, u32[]{:S(2)}) collective-permute-start(bf16[512,1280]{1,0:T(8,128)(2,1)S(1)} %collective-permute-done.refs_14_.refs_9_.refs_11_), channel_id=1, source_target_pairs={{0,48},{16,0},{32,16},{48,32},{8,24},{24,40},{40,56},{56,8},{1,49}... | collective-permute-start | bytes 3932168 | tf_op jit(solution)/shard_map/ppermute | solution.py:23
  76.1 31.1 %collective-permute-start.11 = (bf16[512,1280]{1,0:T(8,128)(2,1)S(1)}, bf16[512,1280]{1,0:T(8,128)(2,1)S(1)}, u32[]{:S(2)}, u32[]{:S(2)}) collective-permute-start(bf16[512,1280]{1,0:T(8,128)(2,1)S(1)} %collective-permute-done.6.refs_15_.refs_10_.refs_12_), channel_id=1, source_target_pairs={{0,16},{16,32},{32,48},{48,0},{8,56},{24,8},{40,24},{56,40},{1,17}... | collective-permute-start | bytes 3932168 | tf_op jit(solution)/shard_map/ppermute | solution.py:23
  78.4 25.0 %collective-permute-start.13 = (bf16[512,1024]{1,0:T(8,128)(2,1)S(1)}, bf16[512,1024]{1,0:T(8,128)(2,1)S(1)}, u32[]{:S(2)}, u32[]{:S(2)}) collective-permute-start(bf16[512,1024]{1,0:T(8,128)(2,1)S(1)} %get-tuple-element.65), channel_id=1, source_target_pairs={{0,1},{1,0},{2,3},{3,2},{4,5},{5,4},{6,7},{7,6},{8,9},{9,8},{10,11... | collective-permute-start | bytes 3145736 | tf_op jit(solution)/shard_map/ppermute | solution.py:27
  90.0 16.0 %collective-permute-start.14 = (bf16[512,1024]{1,0:T(8,128)(2,1)S(1)}, bf16[512,1024]{1,0:T(8,128)(2,1)S(1)}, u32[]{:S(2)}, u32[]{:S(2)}) collective-permute-start(bf16[512,1024]{1,0:T(8,128)(2,1)S(1)} %collective-permute-done.9.refs_6_), channel_id=1, source_target_pairs={{0,2},{2,4},{4,6},{6,0},{8,14},{10,8},{12,10},{14,12},{1,3},{3,5},... | collective-permute-start | bytes 3145736 | tf_op jit(solution)/shard_map/ppermute | solution.py:23
  107.2 12.4 %collective-permute-start.20 = (bf16[1536,1280]{1,0:T(8,128)(2,1)}, bf16[1536,1280]{1,0:T(8,128)(2,1)}, u32[]{:S(2)}, u32[]{:S(2)}) collective-permute-start(bf16[1536,1280]{1,0:T(8,128)(2,1)} %pad_maximum_fusion.1), channel_id=1, source_target_pairs={{0,8},{8,0},{1,9},{9,1},{2,10},{10,2},{3,11},{11,3},{4,12},{12,4},... | collective-permute-start | bytes 11796488 | tf_op jit(solution)/shard_map/ppermute | solution.py:27
  110.5 33.1 %collective-permute-start.16 = (bf16[512,1024]{1,0:T(8,128)(2,1)}, bf16[512,1024]{1,0:T(8,128)(2,1)S(1)}, u32[]{:S(2)}, u32[]{:S(2)}) collective-permute-start(bf16[512,1024]{1,0:T(8,128)(2,1)} %copy-done.25), channel_id=1, source_target_pairs={{0,2},{2,4},{4,6},{6,0},{8,14},{10,8},{12,10},{14,12},{1,3},{3,5},... | collective-permute-start | bytes 3145736 | tf_op jit(solution)/shard_map/ppermute | solution.py:23
  111.8 31.8 %collective-permute-start.17 = (bf16[512,1024]{1,0:T(8,128)(2,1)}, bf16[512,1024]{1,0:T(8,128)(2,1)S(1)}, u32[]{:S(2)}, u32[]{:S(2)}) collective-permute-start(bf16[512,1024]{1,0:T(8,128)(2,1)} %copy-done.24), channel_id=1, source_target_pairs={{0,6},{2,0},{4,2},{6,4},{8,10},{10,12},{12,14},{14,8},{1,7},{3,1},... | collective-permute-start | bytes 3145736 | tf_op jit(solution)/shard_map/ppermute | solution.py:23
  114.8 28.8 %collective-permute-start.18 = (bf16[256,1024]{1,0:T(8,128)(2,1)S(1)}, bf16[256,1024]{1,0:T(8,128)(2,1)S(1)}, u32[]{:S(2)}, u32[]{:S(2)}) collective-permute-start(bf16[256,1024]{1,0:T(8,128)(2,1)S(1)} %slice.48), channel_id=1, source_target_pairs={{0,2},{2,4},{4,6},{6,0},{8,14},{10,8},{12,10},{14,12},{1,3},{3,5},... | collective-permute-start | bytes 1572872 | tf_op jit(solution)/shard_map/ppermute | solution.py:23
  118.4 25.2 %collective-permute-start.19 = (bf16[512,1024]{1,0:T(8,128)(2,1)S(1)}, bf16[512,1024]{1,0:T(8,128)(2,1)S(1)}, u32[]{:S(2)}, u32[]{:S(2)}) collective-permute-start(bf16[512,1024]{1,0:T(8,128)(2,1)S(1)} %copy-done.12), channel_id=1, source_target_pairs={{0,1},{1,0},{2,3},{3,2},{4,5},{5,4},{6,7},{7,6},{8,9},{9,8},{10,11... | collective-permute-start | bytes 3145736 | tf_op jit(solution)/shard_map/ppermute | solution.py:27
  146.6 19.1 %collective-permute-start.22 = (bf16[256,1024]{1,0:T(8,128)(2,1)}, bf16[256,1024]{1,0:T(8,128)(2,1)S(1)}, u32[]{:S(2)}, u32[]{:S(2)}) collective-permute-start(bf16[256,1024]{1,0:T(8,128)(2,1)} %copy-done.29), channel_id=1, source_target_pairs={{0,2},{2,4},{4,6},{6,0},{8,14},{10,8},{12,10},{14,12},{1,3},{3,5},... | collective-permute-start | bytes 1572872 | tf_op jit(solution)/shard_map/ppermute | solution.py:23
  148.3 17.4 %collective-permute-start.23 = (bf16[256,1024]{1,0:T(8,128)(2,1)S(1)}, bf16[256,1024]{1,0:T(8,128)(2,1)}, u32[]{:S(2)}, u32[]{:S(2)}) collective-permute-start(bf16[256,1024]{1,0:T(8,128)(2,1)S(1)} %slice.48), channel_id=1, source_target_pairs={{0,6},{2,0},{4,2},{6,4},{8,10},{10,12},{12,14},{14,8},{1,7},{3,1},... | collective-permute-start | bytes 1572872 | tf_op jit(solution)/shard_map/ppermute | solution.py:23
  149.9 15.9 %collective-permute-start.24 = (bf16[256,1024]{1,0:T(8,128)(2,1)S(1)}, bf16[256,1024]{1,0:T(8,128)(2,1)}, u32[]{:S(2)}, u32[]{:S(2)}) collective-permute-start(bf16[256,1024]{1,0:T(8,128)(2,1)S(1)} %copy-done.13), channel_id=1, source_target_pairs={{0,1},{1,0},{2,3},{3,2},{4,5},{5,4},{6,7},{7,6},{8,9},{9,8},{10,11... | collective-permute-start | bytes 1572872 | tf_op jit(solution)/shard_map/ppermute | solution.py:27
  (33 other events, 508.0 us)

commit v3 on v2

--- a/solution.py
+++ b/solution.py
@@ -32,17 +32,21 @@
     return jnp.sum(wide * wide, axis=-1)
 
 
+def behind(a, *others):
+    return lax.optimization_barrier((a, *others))[0]
+
+
 def together(*arrays):
     return lax.optimization_barrier(arrays)
 
 
-def attend_block(acc, inv, length, out_ref):
+def attend_block(acc, base, inv, length, out_ref):
     span = acc.shape[0]
     half = span // 2
     factor = LOG2E * HEAD**-0.5
     at_k, at_v = GROUPS * HEAD, (GROUPS + 1) * HEAD
-    k = (acc[:, at_k : at_k + HEAD] * inv).astype(jnp.bfloat16)
-    v = (acc[:, at_v : at_v + HEAD] * inv).astype(jnp.bfloat16)
+    k = ((acc[:, at_k : at_k + HEAD] + base[:, at_k : at_k + HEAD]) * inv).astype(jnp.bfloat16)
+    v = ((acc[:, at_v : at_v + HEAD] + base[:, at_v : at_v + HEAD]) * inv).astype(jnp.bfloat16)
     v = jnp.concatenate([v, jnp.ones_like(v)], axis=1)
     for part in range(2):
         lo, hi = part * half, (part + 1) * half
@@ -51,7 +55,7 @@
         bias = jnp.where((col <= row) & (col < length), 0.0, -jnp.inf)
         for g in range(GROUPS):
             at = slice(g * HEAD, (g + 1) * HEAD)
-            q = (acc[lo:hi, at] * inv[lo:hi]).astype(jnp.bfloat16)
+            q = ((acc[lo:hi, at] + base[lo:hi, at]) * inv[lo:hi]).astype(jnp.bfloat16)
             s = lax.dot_general(
                 q, k[:hi], (((1,), (1,)), ((), ())), preferred_element_type=jnp.float32
             )
@@ -118,11 +122,9 @@
 
         fetch(0, 0)
         if acc_ref is not None:
-            load = pltpu.make_async_copy(acc_ref.at[pl.ds(acc_in[1], rows)], acc, sem_c)
+            load = pltpu.make_async_copy(acc_ref.at[pl.ds(acc_in[1], rows)], refs[-1], sem_c)
             load.start()
-            load.wait()
-        else:
-            acc[...] = jnp.zeros_like(acc)
+        acc[...] = jnp.zeros_like(acc)
 
         def step(k, carry):
             slot = lax.rem(k, 2)
@@ -143,7 +145,12 @@
             save = pltpu.make_async_copy(acc, out_ref, sem_c)
         else:
             done = refs[6]
-            attend_block(acc, inv_ref[...], length_ref[0], done)
+            load.wait()
+            columns = []
+            for i in range(out_row // HEAD, (out_row + rows) // HEAD):
+                row = lax.rsqrt(inv_ref[i : i + 1, :] / (GROUPS * feats) + EPS)
+                columns.append(jnp.transpose(jnp.broadcast_to(row, (HEAD, HEAD)))[:, :1])
+            attend_block(acc, refs[-1], jnp.concatenate(columns, axis=0), length_ref[0], done)
             save = pltpu.make_async_copy(done, out_ref.at[pl.ds(out_row, rows)], sem_c)
         save.start()
         save.wait()
@@ -166,7 +173,7 @@
     else:
         specs += [pl.BlockSpec(memory_space=pltpu.VMEM), smem]
         out = jax.ShapeDtypeStruct((2 * rows, GROUPS * HEAD), jnp.bfloat16)
-        scratch.append(pltpu.VMEM((rows, GROUPS * HEAD), jnp.bfloat16))
+        scratch += [pltpu.VMEM((rows, GROUPS * HEAD), jnp.bfloat16), pltpu.VMEM((rows, width), jnp.float32)]
         flops += 6 * 10**9
         if out_old is not None:
             aliases[len(specs)] = 0
@@ -197,6 +204,15 @@
 
     half = span // 2
     h0, w0 = hidden, own
+    def choose(side, *ones):
+        step = jnp.array([k for k, _ in ones], jnp.int32)
+        other = jnp.array([z for _, z in ones], jnp.int32)
+        b = 2 * (jnp.where(c == 0, y - step, y + step) & 3) + (side ^ other)
+        z_at, x_at = b >> 2, b & 3
+        core = jnp.array([0, 1], jnp.int32)[None, :]
+        k = jnp.where(core == 0, x - x_at[:, None], x_at[:, None] - x) & 3
+        return (((z_at ^ zh)[:, None]) * 8 + (core ^ c) * 4 + k).reshape(-1)
+
     f0 = swap(w0, "zh")
     w1, w3 = ring(w0, "x"), ring(w0, "x", -1)
     h1 = ring(h0, "y")
@@ -208,7 +224,7 @@
     h3_hi = ring(h_hi, "y", -1)
     h2_lo = ring(h1[:span], "y")
     lo0 = swap(h_lo, "zl")
-    others = jnp.concatenate([w0, w1, w3], axis=0)
+    others = jnp.concatenate([w0, w1, w3, f0], axis=0)
     square += squares(h1)
     h1_hi = h1[span:]
     w2, f0, f1, h0, h1, h1_hi, h2_lo, h3_hi, lo0, h_hi, square, others = together(
@@ -219,14 +235,19 @@
     h2_hi = ring(h1_hi, "y")
     hi0 = swap(h_hi, "zl")
     lo1 = ring(lo0, "y")
-    more = jnp.concatenate([w2, f0, f1], axis=0)
+    more = jnp.concatenate([w2, f1], axis=0)
+    side = behind(zl, h2_hi)
+    picks = [
+        choose(side, (0, 0), (1, 0), (2, 0), (3, 0), (0, 1)),
+        choose(side, (1, 1), (2, 1), (3, 1)),
+        choose(side, (1, 1), (3, 1), (2, 1)),
+    ]
     square += jnp.concatenate([squares(h2_lo) + squares(h3_lo), squares(h3_hi)], axis=0)
     tail = jnp.concatenate([h1_hi[:half], h3_hi[:half]], axis=0)
-    f3, f2, h2_lo, h2_hi, h3_hi, hi0, lo0, lo1, tail, square, others, more = together(
-        f3, f2, h2_lo, h2_hi, h3_hi, hi0, lo0, lo1, tail, square, others, more
+    f3, f2, h2_lo, h2_hi, h3_hi, hi0, lo0, lo1, tail, square, others, more, *picks = together(
+        f3, f2, h2_lo, h2_hi, h3_hi, hi0, lo0, lo1, tail, square, others, more, *picks
     )
-    more = swap(more, "c")
-    last = swap(jnp.concatenate([f2, f3], axis=0), "c")
+    g2, g3, more = swap(f2, "c"), swap(f3, "c"), swap(more, "c")
     lo2, lo3 = ring(lo1, "y"), ring(lo0, "y", -1)
     mid0 = hi0[half:]
     mid1 = ring(mid0, "y")
@@ -234,31 +255,21 @@
     square += jnp.concatenate([jnp.zeros_like(square[:span]), squares(h2_hi)], axis=0)
     square = square.reshape(8, -1)
     weights = [(w0, 0), (w1, 0), (w2, 0), (w3, 0), (others, 0), (others, rows), (more, 0), (others, 2 * rows)]
-    weights += [(f0, 0), (f1, 0), (f2, 0), (f3, 0), (more, rows), (more, 2 * rows), (last, 0), (last, rows)]
-
-    def choose(*ones):
-        step = jnp.array([k for k, _ in ones], jnp.int32)
-        other = jnp.array([z for _, z in ones], jnp.int32)
-        b = 2 * (jnp.where(c == 0, y - step, y + step) & 3) + (zl ^ other)
-        z_at, x_at = b >> 2, b & 3
-        core = jnp.array([0, 1], jnp.int32)[None, :]
-        k = jnp.where(core == 0, x - x_at[:, None], x_at[:, None] - x) & 3
-        return (((z_at ^ zh)[:, None]) * 8 + (core ^ c) * 4 + k).reshape(-1)
+    weights += [(f0, 0), (f1, 0), (f2, 0), (f3, 0), (others, 3 * rows), (more, rows), (g2, 0), (g3, 0)]
 
     parts = [(h0, 0, 2 * span)], [(h1, 0, 2 * span)], [(h2_lo, 0, span), (h2_hi, 0, span)], [(h3_lo, 0, span), (h3_hi, 0, span)]
     parts += ([(lo0, 0, span), (hi0, 0, span)],)
-    acc = stage(parts, choose((0, 0), (1, 0), (2, 0), (3, 0), (0, 1)), weights)
+    acc = stage(parts, picks[0], weights)
     tail = h2_hi[:half]
     lo2, lo3, mid0, mid1, tails, tail, acc, square = together(lo2, lo3, mid0, mid1, tails, tail, acc, square)
-    square = square + swap(square, "zl")
+    square += swap(square, "zl")
     mid2, mid3 = ring(mid1, "y"), ring(mid0, "y", -1)
     tail2 = swap(tail, "zl")
-    inv = lax.rsqrt(square.reshape(-1, 1) / (feats * 8) + EPS)
     parts = [(lo1, 0, span)], [(lo2, 0, span)], [(lo3, 0, span)]
-    out = stage(parts, choose((1, 1), (2, 1), (3, 1)), weights, (acc, 0), (inv[:span], lengths[:1], 0, None))
+    out = stage(parts, picks[1], weights, (acc, 0), (square, lengths[:1], 0, None))
     mid2, mid3, tail2, out = together(mid2, mid3, tail2, out)
     parts = [(tails, 0, half), (mid1, 0, half)], [(tails, half, half), (mid3, 0, half)], [(tail2, 0, half), (mid2, 0, half)]
-    return stage(parts, choose((1, 1), (3, 1), (2, 1)), weights, (acc, span), (inv[span:], lengths[1:], span, out))
+    return stage(parts, picks[2], weights, (acc, span), (square, lengths[1:], span, out))
 
 
 def solution(mesh):

time: 180 us -> 177 us (0.983)
  waiting for transfers between devices: 74.5 us -> 60.7 us
  other arithmetic: 10.3 us -> 21.4 us
    ppermute x17, waiting for transfers between devices: 64.5 us -> 44.8 us  [ring(): return lax.ppermute(a, ('c', 'y') if axis == 'y' else ('x', 'c'), perm)]
    concatenate x3 -> x2, other arithmetic: 2.7 us -> 13.2 us  [the longest x1 11.7 us: local(): others = jnp.concatenate([w0, w1, w3, f0], axis=0)]
    ppermute x9 -> x10, waiting for transfers between devices: 10 us -> 15.9 us  [swap(): return lax.ppermute(a, axis, [(0, 1), (1, 0)])]
    unnamed x63 -> x51, local copies, waits for them, and re-layouts: 3.93 us -> 5.02 us
    ppermute x9 -> x10, starting transfers between devices: 9.54 us -> 10.1 us  [swap(): return lax.ppermute(a, axis, [(0, 1), (1, 0)])]
  transfers between devices with their start and end apart: 26 -> 27, of which waited for: 12 -> 13; matrix products, arithmetic and copies ran while one was open for 12% -> 19% of each run, Pallas kernels for 18% -> 18%
where the time goes in v3:
time: 177 us
  waiting for transfers between devices  60.7 us (34%)
  Pallas kernels  44.3 us (25%)
  starting transfers between devices  34.3 us (19%)
  other arithmetic  21.4 us (12%)
  local copies, waits for them, and re-layouts  15.5 us (9%)
    ppermute x17, waiting for transfers between devices, ring(): return lax.ppermute(a, ('c', 'y') if axis == 'y' else ('x', 'c'), perm)  44.8 us
    pallas_call x3, Pallas kernels, stage(): pl.pallas_call(body, in_specs=specs, out_specs=main, out_shape=out, scrat...  44.3 us
    ppermute x17, starting transfers between devices, ring(): return lax.ppermute(a, ('c', 'y') if axis == 'y' else ('x', 'c'), perm)  24.2 us
    ppermute x10, waiting for transfers between devices, swap(): return lax.ppermute(a, axis, [(0, 1), (1, 0)])  15.9 us
    concatenate x1, other arithmetic, local(): others = jnp.concatenate([w0, w1, w3, f0], axis=0)  11.7 us
    ppermute x10, starting transfers between devices, swap(): return lax.ppermute(a, axis, [(0, 1), (1, 0)])  10.1 us
    unnamed x51, local copies, waits for them, and re-layouts  5.02 us
    reduce_sum x5, other arithmetic, squares(): return jnp.sum(wide * wide, axis=-1)  4.81 us
  transfers between devices with their start and end apart: 27, of which 13 were waited for; matrix products, arithmetic and copies ran while one was open for 19% of the time, Pallas kernels for 18%

profile of v3, /device:TPU:0, one launch (start us, length us, event | category | flops | bytes accessed | tf_op | source)
XLA Modules:
  0.0 176.7 jit_solution(10334480021163694450)
XLA Ops:
  0.0 1.7 collective-permute-start.3
  4.9 4.0 %collective-permute-start = (bf16[512,1280]{1,0:T(8,128)(2,1)S(1)}, bf16[512,1280]{1,0:T(8,128)(2,1)}, u32[]{:S(2)}, u32[]{:S(2)}) collective-permute-start(bf16[512,1280]{1,0:T(8,128)(2,1)S(1)} %multiply_convert_fusion.refs_8_.refs_3_.refs_5_), channel_id=1, source_target_pairs={{0,64},{64,0},{1,65},{65,1},{2,66},{66,2},{3,67},{67,3},{4,68},{68... | collective-permute-start | bytes 3932168 | tf_op jit(solution)/shard_map/ppermute | solution.py:27
  10.4 1.7 collective-permute-start.2
  13.3 1.8 %collective-permute-start.4 = (bf16[512,1024]{1,0:T(8,128)(2,1)S(1)}, bf16[512,1024]{1,0:T(8,128)(2,1)S(1)}, u32[]{:S(2)}, u32[]{:S(2)}) collective-permute-start(bf16[512,1024]{1,0:T(8,128)(2,1)S(1)} %get-tuple-element.60), channel_id=1, source_target_pairs={{0,6},{2,0},{4,2},{6,4},{8,10},{10,12},{12,14},{14,8},{1,7},{3,1},... | collective-permute-start | bytes 3145736 | tf_op jit(solution)/shard_map/ppermute | solution.py:23
  15.5 21.4 %collective-permute-done.4.refs_4_ = bf16[512,1024]{1,0:T(8,128)(2,1)S(1)} collective-permute-done((bf16[512,1024]{1,0:T(8,128)(2,1)S(1)}, bf16[512,1024]{1,0:T(8,128)(2,1)S(1)}, u32[]{:S(2)}, u32[]{:S(2)}) %collective-permute-start.4) | collective-permute-done | bytes 1048608 | tf_op jit(solution)/shard_map/ppermute | solution.py:23
  41.8 1.8 %collective-permute-start.6 = (bf16[512,1280]{1,0:T(8,128)(2,1)}, bf16[512,1280]{1,0:T(8,128)(2,1)}, u32[]{:S(2)}, u32[]{:S(2)}) collective-permute-start(bf16[512,1280]{1,0:T(8,128)(2,1)} %collective-permute-done.refs_14_.refs_9_.refs_11_), channel_id=1, source_target_pairs={{0,16},{16,32},{32,48},{48,0},{8,56},{24,8},{40,24},{56,40},{1,17}... | collective-permute-start | bytes 3932168 | tf_op jit(solution)/shard_map/ppermute | solution.py:23
  43.6 2.7 %fusion.13 = (bf16[512,1024]{1,0:T(8,128)(2,1)S(1)}, bf16[512,1024]{1,0:T(8,128)(2,1)}) fusion(bf16[1024,1024]{1,0:T(8,128)(2,1)} %collective-permute-done.3.refs_1_), kind=kLoop, calls=%fused_computation.40 | loop fusion | bytes 4194304 | tf_op jit(solution)/shard_map/slice | solution.py:225
  46.8 2.8 %collective-permute-start.8 = (bf16[512,1024]{1,0:T(8,128)(2,1)}, bf16[512,1024]{1,0:T(8,128)(2,1)S(1)}, u32[]{:S(2)}, u32[]{:S(2)}) collective-permute-start(bf16[512,1024]{1,0:T(8,128)(2,1)} %get-tuple-element.69), channel_id=1, source_target_pairs={{0,6},{2,0},{4,2},{6,4},{8,10},{10,12},{12,14},{14,8},{1,7},{3,1},... | collective-permute-start | bytes 3145736 | tf_op jit(solution)/shard_map/ppermute | solution.py:23
  50.6 2.1 %multiply_reduce_fusion = f32[1024]{0:T(1024)S(1)} fusion(bf16[1024,1024]{1,0:T(8,128)(2,1)} %collective-permute-done.3.refs_1_), kind=kLoop, calls=%fused_computation.1 | loop fusion | flops 3144704 | bytes 2101248 | tf_op jit(solution)/shard_map/reduce_sum | solution.py:32
  52.7 11.7 %pad_maximum_fusion = bf16[2048,1280]{1,0:T(8,128)(2,1)} fusion(bf16[512,1280]{1,0:T(8,128)(2,1)} %collective-permute-done.refs_14_.refs_9_.refs_11_, bf16[512,1280]{1,0:T(8,128)(2,1)S(1)} %collective-permute-done.2.refs_11_.refs_6_.refs_8_, bf16[512,1280]{1,0:T(8,128)(2,1)S(1)} %collective-permute-done.1.refs_9_.refs_4_.refs_6_, ...), kind=kLoop, calls=%fused_computation | loop fusion | flops 20971520 | bytes 10485760 | tf_op jit(solution)/shard_map/concatenate | solution.py:227
  64.3 8.5 %collective-permute-done.7.refs_2_ = bf16[512,1024]{1,0:T(8,128)(2,1)S(1)} collective-permute-done((bf16[512,1024]{1,0:T(8,128)(2,1)S(1)}, bf16[512,1024]{1,0:T(8,128)(2,1)S(1)}, u32[]{:S(2)}, u32[]{:S(2)}) %collective-permute-start.7) | collective-permute-done | bytes 1048608 | tf_op jit(solution)/shard_map/ppermute | solution.py:23
  74.3 2.0 %collective-permute-start.12 = (bf16[512,1024]{1,0:T(8,128)(2,1)}, bf16[512,1024]{1,0:T(8,128)(2,1)}, u32[]{:S(2)}, u32[]{:S(2)}) collective-permute-start(bf16[512,1024]{1,0:T(8,128)(2,1)} %get-tuple-element.67), channel_id=1, source_target_pairs={{0,2},{2,4},{4,6},{6,0},{8,14},{10,8},{12,10},{14,12},{1,3},{3,5},... | collective-permute-start | bytes 3145736 | tf_op jit(solution)/shard_map/ppermute | solution.py:23
  77.7 2.0 %collective-permute-start.11 = (bf16[512,1280]{1,0:T(8,128)(2,1)}, bf16[512,1280]{1,0:T(8,128)(2,1)}, u32[]{:S(2)}, u32[]{:S(2)}) collective-permute-start(bf16[512,1280]{1,0:T(8,128)(2,1)} %collective-permute-done.6.refs_15_.refs_10_.refs_12_), channel_id=1, source_target_pairs={{0,16},{16,32},{32,48},{48,0},{8,56},{24,8},{40,24},{56,40},{1,17}... | collective-permute-start | bytes 3932168 | tf_op jit(solution)/shard_map/ppermute | solution.py:23
  83.9 6.7 %collective-permute-done.12.refs_3_ = bf16[512,1024]{1,0:T(8,128)(2,1)} collective-permute-done((bf16[512,1024]{1,0:T(8,128)(2,1)}, bf16[512,1024]{1,0:T(8,128)(2,1)}, u32[]{:S(2)}, u32[]{:S(2)}) %collective-permute-start.12) | collective-permute-done | bytes 1048608 | tf_op jit(solution)/shard_map/ppermute | solution.py:23
  93.6 11.8 %collective-permute-done.13.refs_7_ = bf16[512,1024]{1,0:T(8,128)(2,1)} collective-permute-done((bf16[512,1024]{1,0:T(8,128)(2,1)}, bf16[512,1024]{1,0:T(8,128)(2,1)}, u32[]{:S(2)}, u32[]{:S(2)}) %collective-permute-start.13) | collective-permute-done | bytes 1048608 | tf_op jit(solution)/shard_map/ppermute | solution.py:27
  105.4 1.6 collective-permute-done.14.refs_0_
  107.0 2.7 %collective-permute-done.10.refs_17_.refs_12_.refs_14_ = bf16[512,1280]{1,0:T(8,128)(2,1)} collective-permute-done((bf16[512,1280]{1,0:T(8,128)(2,1)}, bf16[512,1280]{1,0:T(8,128)(2,1)}, u32[]{:S(2)}, u32[]{:S(2)}) %collective-permute-start.10) | collective-permute-done | bytes 1310752 | tf_op jit(solution)/shard_map/ppermute | solution.py:23
  111.0 2.5 %collective-permute-start.17 = (bf16[512,1024]{1,0:T(8,128)(2,1)}, bf16[512,1024]{1,0:T(8,128)(2,1)}, u32[]{:S(2)}, u32[]{:S(2)}) collective-permute-start(bf16[512,1024]{1,0:T(8,128)(2,1)} %collective-permute-done.9.refs_6_), channel_id=1, source_target_pairs={{0,6},{2,0},{4,2},{6,4},{8,10},{10,12},{12,14},{14,8},{1,7},{3,1},... | collective-permute-start | bytes 3145736 | tf_op jit(solution)/shard_map/ppermute | solution.py:23
  120.1 1.6 copy-done.18
  121.7 20.0 %shard_map.136.refs_15_.refs_17_ = f32[1024,1280]{1,0:T(8,128)} custom-call(s32[10]{0:T(128)} %add.125.sel_ref, bf16[1024,1024]{1,0:T(8,128)(2,1)} %refs_0_, bf16[1024,1024]{1,0:T(8,128)(2,1)} %collective-permute-done.3.refs_1_, bf16[512,1024]{1,0:T(8,128)(2,1)} %copy-done.8, bf16[512,1024]{1,0:T(8,128)(2,1)} %collective-permute-done.12.refs_3_, ...), custom_call_target="tpu_custom_call" | custom-call | flops 13421772800 | bytes 20000000 | tf_op jit(solution)/shard_map/pallas_call | solution.py:181
  141.7 1.6 collective-permute-done.18.refs_1_
  146.4 3.1 %collective-permute-start.24 = (bf16[256,1024]{1,0:T(8,128)(2,1)S(1)}, bf16[256,1024]{1,0:T(8,128)(2,1)S(1)}, u32[]{:S(2)}, u32[]{:S(2)}) collective-permute-start(bf16[256,1024]{1,0:T(8,128)(2,1)S(1)} %slice.36), channel_id=1, source_target_pairs={{0,6},{2,0},{4,2},{6,4},{8,10},{10,12},{12,14},{14,8},{1,7},{3,1},... | collective-permute-start | bytes 1572872 | tf_op jit(solution)/shard_map/ppermute | solution.py:23
  151.1 12.2 %shard_map.137.refs_20_ = bf16[1024,1024]{1,0:T(8,128)(2,1)} custom-call(s32[6]{0:T(128)} %add.132.sel_ref, bf16[512,1024]{1,0:T(8,128)(2,1)} %collective-permute-done.14.refs_0_, bf16[512,1024]{1,0:T(8,128)(2,1)} %collective-permute-done.16.refs_1_, bf16[512,1024]{1,0:T(8,128)(2,1)} %collective-permute-done.17.refs_2_, bf16[512,1280]{1,0:T(8,128)(2,1)} %copy-done.1, ...), custom_call_target="tpu_custom_call" | custom-call | flops 10026531840 | bytes 12000000 | tf_op jit(solution)/shard_map/pallas_call | solution.py:181
  164.4 12.1 %shard_map.138 = bf16[1024,1024]{1,0:T(8,128)(2,1)} custom-call(s32[6]{0:T(128)} %add.139.sel_ref, bf16[512,1024]{1,0:T(8,128)(2,1)} %collective-permute-done.19.refs_0_, bf16[256,1024]{1,0:T(8,128)(2,1)} %copy-done.21, bf16[256,1024]{1,0:T(8,128)(2,1)} %copy-done.23, bf16[256,1024]{1,0:T(8,128)(2,1)} %copy-done.24, ...), custom_call_target="tpu_custom_call", output_to_operand_aliasing={{}: (21, {})} | custom-call | flops 10026531840 | bytes 12000000 | tf_op jit(solution)/shard_map/pallas_call | solution.py:181
  (118 shorter events, 36.0 us)
Async XLA Ops:
  0.0 40.6 %collective-permute-start.3 = (bf16[1024,1024]{1,0:T(8,128)(2,1)}, bf16[1024,1024]{1,0:T(8,128)(2,1)}, u32[]{:S(2)}, u32[]{:S(2)}) collective-permute-start(bf16[1024,1024]{1,0:T(8,128)(2,1)} %refs_0_), channel_id=1, source_target_pairs={{0,2},{2,4},{4,6},{6,0},{8,14},{10,8},{12,10},{14,12},{1,3},{3,5},... | collective-permute-start | bytes 6291464 | tf_op jit(solution)/shard_map/ppermute | solution.py:23
  4.9 33.4 %collective-permute-start = (bf16[512,1280]{1,0:T(8,128)(2,1)S(1)}, bf16[512,1280]{1,0:T(8,128)(2,1)}, u32[]{:S(2)}, u32[]{:S(2)}) collective-permute-start(bf16[512,1280]{1,0:T(8,128)(2,1)S(1)} %multiply_convert_fusion.refs_8_.refs_3_.refs_5_), channel_id=1, source_target_pairs={{0,64},{64,0},{1,65},{65,1},{2,66},{66,2},{3,67},{67,3},{4,68},{68... | collective-permute-start | bytes 3932168 | tf_op jit(solution)/shard_map/ppermute | solution.py:27
  8.9 30.6 %collective-permute-start.1 = (bf16[512,1280]{1,0:T(8,128)(2,1)S(1)}, bf16[512,1280]{1,0:T(8,128)(2,1)S(1)}, u32[]{:S(2)}, u32[]{:S(2)}) collective-permute-start(bf16[512,1280]{1,0:T(8,128)(2,1)S(1)} %multiply_convert_fusion.refs_8_.refs_3_.refs_5_), channel_id=1, source_target_pairs={{0,16},{16,32},{32,48},{48,0},{8,56},{24,8},{40,24},{56,40},{1,17}... | collective-permute-start | bytes 3932168 | tf_op jit(solution)/shard_map/ppermute | solution.py:23
  10.4 30.2 %collective-permute-start.2 = (bf16[512,1280]{1,0:T(8,128)(2,1)S(1)}, bf16[512,1280]{1,0:T(8,128)(2,1)S(1)}, u32[]{:S(2)}, u32[]{:S(2)}) collective-permute-start(bf16[512,1280]{1,0:T(8,128)(2,1)S(1)} %multiply_convert_fusion.refs_8_.refs_3_.refs_5_), channel_id=1, source_target_pairs={{0,48},{16,0},{32,16},{48,32},{8,24},{24,40},{40,56},{56,8},{1,49}... | collective-permute-start | bytes 3932168 | tf_op jit(solution)/shard_map/ppermute | solution.py:23
  13.3 23.7 %collective-permute-start.4 = (bf16[512,1024]{1,0:T(8,128)(2,1)S(1)}, bf16[512,1024]{1,0:T(8,128)(2,1)S(1)}, u32[]{:S(2)}, u32[]{:S(2)}) collective-permute-start(bf16[512,1024]{1,0:T(8,128)(2,1)S(1)} %get-tuple-element.60), channel_id=1, source_target_pairs={{0,6},{2,0},{4,2},{6,4},{8,10},{10,12},{12,14},{14,8},{1,7},{3,1},... | collective-permute-start | bytes 3145736 | tf_op jit(solution)/shard_map/ppermute | solution.py:23
  40.6 32.5 %collective-permute-start.5 = (bf16[512,1280]{1,0:T(8,128)(2,1)S(1)}, bf16[512,1280]{1,0:T(8,128)(2,1)S(1)}, u32[]{:S(2)}, u32[]{:S(2)}) collective-permute-start(bf16[512,1280]{1,0:T(8,128)(2,1)S(1)} %collective-permute-done.1.refs_9_.refs_4_.refs_6_), channel_id=1, source_target_pairs={{0,16},{16,32},{32,48},{48,0},{8,56},{24,8},{40,24},{56,40},{1,17}... | collective-permute-start | bytes 3932168 | tf_op jit(solution)/shard_map/ppermute | solution.py:23
  41.8 32.5 %collective-permute-start.6 = (bf16[512,1280]{1,0:T(8,128)(2,1)}, bf16[512,1280]{1,0:T(8,128)(2,1)}, u32[]{:S(2)}, u32[]{:S(2)}) collective-permute-start(bf16[512,1280]{1,0:T(8,128)(2,1)} %collective-permute-done.refs_14_.refs_9_.refs_11_), channel_id=1, source_target_pairs={{0,16},{16,32},{32,48},{48,0},{8,56},{24,8},{40,24},{56,40},{1,17}... | collective-permute-start | bytes 3932168 | tf_op jit(solution)/shard_map/ppermute | solution.py:23
  46.3 26.6 %collective-permute-start.7 = (bf16[512,1024]{1,0:T(8,128)(2,1)S(1)}, bf16[512,1024]{1,0:T(8,128)(2,1)S(1)}, u32[]{:S(2)}, u32[]{:S(2)}) collective-permute-start(bf16[512,1024]{1,0:T(8,128)(2,1)S(1)} %get-tuple-element.111), channel_id=1, source_target_pairs={{0,2},{2,4},{4,6},{6,0},{8,14},{10,8},{12,10},{14,12},{1,3},{3,5},... | collective-permute-start | bytes 3145736 | tf_op jit(solution)/shard_map/ppermute | solution.py:23
  46.8 26.1 %collective-permute-start.8 = (bf16[512,1024]{1,0:T(8,128)(2,1)}, bf16[512,1024]{1,0:T(8,128)(2,1)S(1)}, u32[]{:S(2)}, u32[]{:S(2)}) collective-permute-start(bf16[512,1024]{1,0:T(8,128)(2,1)} %get-tuple-element.69), channel_id=1, source_target_pairs={{0,6},{2,0},{4,2},{6,4},{8,10},{10,12},{12,14},{14,8},{1,7},{3,1},... | collective-permute-start | bytes 3145736 | tf_op jit(solution)/shard_map/ppermute | solution.py:23
  49.5 23.5 %collective-permute-start.9 = (bf16[512,1024]{1,0:T(8,128)(2,1)S(1)}, bf16[512,1024]{1,0:T(8,128)(2,1)}, u32[]{:S(2)}, u32[]{:S(2)}) collective-permute-start(bf16[512,1024]{1,0:T(8,128)(2,1)S(1)} %get-tuple-element.60), channel_id=1, source_target_pairs={{0,1},{1,0},{2,3},{3,2},{4,5},{5,4},{6,7},{7,6},{8,9},{9,8},{10,11... | collective-permute-start | bytes 3145736 | tf_op jit(solution)/shard_map/ppermute | solution.py:27
  74.3 35.4 %collective-permute-start.15 = (bf16[2048,1280]{1,0:T(8,128)(2,1)}, bf16[2048,1280]{1,0:T(8,128)(2,1)}, u32[]{:S(2)}, u32[]{:S(2)}) collective-permute-start(bf16[2048,1280]{1,0:T(8,128)(2,1)} %pad_maximum_fusion), channel_id=1, source_target_pairs={{0,8},{8,0},{1,9},{9,1},{2,10},{10,2},{3,11},{11,3},{4,12},{12,4},... | collective-permute-start | bytes 15728648 | tf_op jit(solution)/shard_map/ppermute | solution.py:27
  74.3 16.4 %collective-permute-start.12 = (bf16[512,1024]{1,0:T(8,128)(2,1)}, bf16[512,1024]{1,0:T(8,128)(2,1)}, u32[]{:S(2)}, u32[]{:S(2)}) collective-permute-start(bf16[512,1024]{1,0:T(8,128)(2,1)} %get-tuple-element.67), channel_id=1, source_target_pairs={{0,2},{2,4},{4,6},{6,0},{8,14},{10,8},{12,10},{14,12},{1,3},{3,5},... | collective-permute-start | bytes 3145736 | tf_op jit(solution)/shard_map/ppermute | solution.py:23
  77.7 32.0 %collective-permute-start.10 = (bf16[512,1280]{1,0:T(8,128)(2,1)}, bf16[512,1280]{1,0:T(8,128)(2,1)}, u32[]{:S(2)}, u32[]{:S(2)}) collective-permute-start(bf16[512,1280]{1,0:T(8,128)(2,1)} %collective-permute-done.refs_14_.refs_9_.refs_11_), channel_id=1, source_target_pairs={{0,48},{16,0},{32,16},{48,32},{8,24},{24,40},{40,56},{56,8},{1,49}... | collective-permute-start | bytes 3932168 | tf_op jit(solution)/shard_map/ppermute | solution.py:23
  77.7 31.9 %collective-permute-start.11 = (bf16[512,1280]{1,0:T(8,128)(2,1)}, bf16[512,1280]{1,0:T(8,128)(2,1)}, u32[]{:S(2)}, u32[]{:S(2)}) collective-permute-start(bf16[512,1280]{1,0:T(8,128)(2,1)} %collective-permute-done.6.refs_15_.refs_10_.refs_12_), channel_id=1, source_target_pairs={{0,16},{16,32},{32,48},{48,0},{8,56},{24,8},{40,24},{56,40},{1,17}... | collective-permute-start | bytes 3932168 | tf_op jit(solution)/shard_map/ppermute | solution.py:23
  79.8 25.7 %collective-permute-start.13 = (bf16[512,1024]{1,0:T(8,128)(2,1)}, bf16[512,1024]{1,0:T(8,128)(2,1)}, u32[]{:S(2)}, u32[]{:S(2)}) collective-permute-start(bf16[512,1024]{1,0:T(8,128)(2,1)} %get-tuple-element.69), channel_id=1, source_target_pairs={{0,1},{1,0},{2,3},{3,2},{4,5},{5,4},{6,7},{7,6},{8,9},{9,8},{10,11... | collective-permute-start | bytes 3145736 | tf_op jit(solution)/shard_map/ppermute | solution.py:27
  90.7 16.3 %collective-permute-start.14 = (bf16[512,1024]{1,0:T(8,128)(2,1)}, bf16[512,1024]{1,0:T(8,128)(2,1)}, u32[]{:S(2)}, u32[]{:S(2)}) collective-permute-start(bf16[512,1024]{1,0:T(8,128)(2,1)} %collective-permute-done.9.refs_6_), channel_id=1, source_target_pairs={{0,2},{2,4},{4,6},{6,0},{8,14},{10,8},{12,10},{14,12},{1,3},{3,5},... | collective-permute-start | bytes 3145736 | tf_op jit(solution)/shard_map/ppermute | solution.py:23
  109.7 10.4 %collective-permute-start.20 = (bf16[1024,1280]{1,0:T(8,128)(2,1)S(1)}, bf16[1024,1280]{1,0:T(8,128)(2,1)S(1)}, u32[]{:S(2)}, u32[]{:S(2)}) collective-permute-start(bf16[1024,1280]{1,0:T(8,128)(2,1)S(1)} %pad_maximum_fusion.1), channel_id=1, source_target_pairs={{0,8},{8,0},{1,9},{9,1},{2,10},{10,2},{3,11},{11,3},{4,12},{12,4},... | collective-permute-start | bytes 7864328 | tf_op jit(solution)/shard_map/ppermute | solution.py:27
  110.3 33.1 %collective-permute-start.16 = (bf16[512,1024]{1,0:T(8,128)(2,1)}, bf16[512,1024]{1,0:T(8,128)(2,1)}, u32[]{:S(2)}, u32[]{:S(2)}) collective-permute-start(bf16[512,1024]{1,0:T(8,128)(2,1)} %collective-permute-done.14.refs_0_), channel_id=1, source_target_pairs={{0,2},{2,4},{4,6},{6,0},{8,14},{10,8},{12,10},{14,12},{1,3},{3,5},... | collective-permute-start | bytes 3145736 | tf_op jit(solution)/shard_map/ppermute | solution.py:23
  111.0 32.4 %collective-permute-start.17 = (bf16[512,1024]{1,0:T(8,128)(2,1)}, bf16[512,1024]{1,0:T(8,128)(2,1)}, u32[]{:S(2)}, u32[]{:S(2)}) collective-permute-start(bf16[512,1024]{1,0:T(8,128)(2,1)} %collective-permute-done.9.refs_6_), channel_id=1, source_target_pairs={{0,6},{2,0},{4,2},{6,4},{8,10},{10,12},{12,14},{14,8},{1,7},{3,1},... | collective-permute-start | bytes 3145736 | tf_op jit(solution)/shard_map/ppermute | solution.py:23
  117.2 26.1 %collective-permute-start.18 = (bf16[256,1024]{1,0:T(8,128)(2,1)S(1)}, bf16[256,1024]{1,0:T(8,128)(2,1)S(1)}, u32[]{:S(2)}, u32[]{:S(2)}) collective-permute-start(bf16[256,1024]{1,0:T(8,128)(2,1)S(1)} %slice.36), channel_id=1, source_target_pairs={{0,2},{2,4},{4,6},{6,0},{8,14},{10,8},{12,10},{14,12},{1,3},{3,5},... | collective-permute-start | bytes 1572872 | tf_op jit(solution)/shard_map/ppermute | solution.py:23
  118.6 26.1 %collective-permute-start.19 = (bf16[512,1024]{1,0:T(8,128)(2,1)S(1)}, bf16[512,1024]{1,0:T(8,128)(2,1)}, u32[]{:S(2)}, u32[]{:S(2)}) collective-permute-start(bf16[512,1024]{1,0:T(8,128)(2,1)S(1)} %copy-done.9), channel_id=1, source_target_pairs={{0,1},{1,0},{2,3},{3,2},{4,5},{5,4},{6,7},{7,6},{8,9},{9,8},{10,11... | collective-permute-start | bytes 3145736 | tf_op jit(solution)/shard_map/ppermute | solution.py:27
  146.2 17.0 %collective-permute-start.23 = (bf16[256,1024]{1,0:T(8,128)(2,1)S(1)}, bf16[256,1024]{1,0:T(8,128)(2,1)S(1)}, u32[]{:S(2)}, u32[]{:S(2)}) collective-permute-start(bf16[256,1024]{1,0:T(8,128)(2,1)S(1)} %collective-permute-done.18.refs_1_), channel_id=1, source_target_pairs={{0,2},{2,4},{4,6},{6,0},{8,14},{10,8},{12,10},{14,12},{1,3},{3,5},... | collective-permute-start | bytes 1572872 | tf_op jit(solution)/shard_map/ppermute | solution.py:23
  146.4 16.9 %collective-permute-start.24 = (bf16[256,1024]{1,0:T(8,128)(2,1)S(1)}, bf16[256,1024]{1,0:T(8,128)(2,1)S(1)}, u32[]{:S(2)}, u32[]{:S(2)}) collective-permute-start(bf16[256,1024]{1,0:T(8,128)(2,1)S(1)} %slice.36), channel_id=1, source_target_pairs={{0,6},{2,0},{4,2},{6,4},{8,10},{10,12},{12,14},{14,8},{1,7},{3,1},... | collective-permute-start | bytes 1572872 | tf_op jit(solution)/shard_map/ppermute | solution.py:23
  149.5 13.8 %collective-permute-start.25 = (bf16[256,1024]{1,0:T(8,128)(2,1)S(1)}, bf16[256,1024]{1,0:T(8,128)(2,1)S(1)}, u32[]{:S(2)}, u32[]{:S(2)}) collective-permute-start(bf16[256,1024]{1,0:T(8,128)(2,1)S(1)} %slice.37), channel_id=1, source_target_pairs={{0,1},{1,0},{2,3},{3,2},{4,5},{5,4},{6,7},{7,6},{8,9},{9,8},{10,11... | collective-permute-start | bytes 1572872 | tf_op jit(solution)/shard_map/ppermute | solution.py:27
  (28 other events, 319.2 us)

commit v4 on v3

--- a/solution.py
+++ b/solution.py
@@ -213,8 +213,8 @@
         k = jnp.where(core == 0, x - x_at[:, None], x_at[:, None] - x) & 3
         return (((z_at ^ zh)[:, None]) * 8 + (core ^ c) * 4 + k).reshape(-1)
 
+    w1, w3 = ring(w0, "x"), ring(w0, "x", -1)
     f0 = swap(w0, "zh")
-    w1, w3 = ring(w0, "x"), ring(w0, "x", -1)
     h1 = ring(h0, "y")
     h_lo, h_hi = h0[:span], h0[span:]
     h3_lo = ring(h_lo, "y", -1)
@@ -250,7 +250,7 @@
     g2, g3, more = swap(f2, "c"), swap(f3, "c"), swap(more, "c")
     lo2, lo3 = ring(lo1, "y"), ring(lo0, "y", -1)
     mid0 = hi0[half:]
-    mid1 = ring(mid0, "y")
+    mid1 = ring(behind(mid0, g2), "y")
     tails = swap(tail, "zl")
     square += jnp.concatenate([jnp.zeros_like(square[:span]), squares(h2_hi)], axis=0)
     square = square.reshape(8, -1)

time: 177 us -> 177 us (level)
    ppermute x10, waiting for transfers between devices: 15.9 us -> 13.8 us  [swap(): return lax.ppermute(a, axis, [(0, 1), (1, 0)])]
  transfers between devices with their start and end apart: 27 -> 27, of which waited for: 13 -> 12; matrix products, arithmetic and copies ran while one was open for 19% -> 19% of each run, Pallas kernels for 18% -> 18%
where the time goes in v4:
time: 177 us
  waiting for transfers between devices  59.5 us (34%)
  Pallas kernels  44.3 us (25%)
  starting transfers between devices  34.9 us (20%)
  other arithmetic  21.4 us (12%)
  local copies, waits for them, and re-layouts  16 us (9%)
    ppermute x17, waiting for transfers between devices, ring(): return lax.ppermute(a, ('c', 'y') if axis == 'y' else ('x', 'c'), perm)  45.7 us
    pallas_call x3, Pallas kernels, stage(): pl.pallas_call(body, in_specs=specs, out_specs=main, out_shape=out, scrat...  44.3 us
    ppermute x17, starting transfers between devices, ring(): return lax.ppermute(a, ('c', 'y') if axis == 'y' else ('x', 'c'), perm)  24.8 us
    ppermute x10, waiting for transfers between devices, swap(): return lax.ppermute(a, axis, [(0, 1), (1, 0)])  13.8 us
    concatenate x1, other arithmetic, local(): others = jnp.concatenate([w0, w1, w3, f0], axis=0)  11.7 us
    ppermute x10, starting transfers between devices, swap(): return lax.ppermute(a, axis, [(0, 1), (1, 0)])  10.1 us
    unnamed x51, local copies, waits for them, and re-layouts  5.54 us
    reduce_sum x5, other arithmetic, squares(): return jnp.sum(wide * wide, axis=-1)  4.81 us
  transfers between devices with their start and end apart: 27, of which 12 were waited for; matrix products, arithmetic and copies ran while one was open for 19% of the time, Pallas kernels for 18%

profile of v4, /device:TPU:0, one launch (start us, length us, event | category | flops | bytes accessed | tf_op | source)
XLA Modules:
  0.0 176.5 jit_solution(3144045565355546420)
XLA Ops:
  0.0 1.7 collective-permute-start.3
  4.9 4.0 %collective-permute-start = (bf16[512,1280]{1,0:T(8,128)(2,1)S(1)}, bf16[512,1280]{1,0:T(8,128)(2,1)}, u32[]{:S(2)}, u32[]{:S(2)}) collective-permute-start(bf16[512,1280]{1,0:T(8,128)(2,1)S(1)} %multiply_convert_fusion.refs_8_.refs_3_.refs_5_), channel_id=1, source_target_pairs={{0,64},{64,0},{1,65},{65,1},{2,66},{66,2},{3,67},{67,3},{4,68},{68... | collective-permute-start | bytes 3932168 | tf_op jit(solution)/shard_map/ppermute | solution.py:27
  10.4 1.7 collective-permute-start.2
  13.3 1.8 %collective-permute-start.4 = (bf16[512,1024]{1,0:T(8,128)(2,1)S(1)}, bf16[512,1024]{1,0:T(8,128)(2,1)S(1)}, u32[]{:S(2)}, u32[]{:S(2)}) collective-permute-start(bf16[512,1024]{1,0:T(8,128)(2,1)S(1)} %get-tuple-element.61), channel_id=1, source_target_pairs={{0,6},{2,0},{4,2},{6,4},{8,10},{10,12},{12,14},{14,8},{1,7},{3,1},... | collective-permute-start | bytes 3145736 | tf_op jit(solution)/shard_map/ppermute | solution.py:23
  15.5 21.4 %collective-permute-done.4.refs_4_ = bf16[512,1024]{1,0:T(8,128)(2,1)S(1)} collective-permute-done((bf16[512,1024]{1,0:T(8,128)(2,1)S(1)}, bf16[512,1024]{1,0:T(8,128)(2,1)S(1)}, u32[]{:S(2)}, u32[]{:S(2)}) %collective-permute-start.4) | collective-permute-done | bytes 1048608 | tf_op jit(solution)/shard_map/ppermute | solution.py:23
  41.8 1.8 %collective-permute-start.6 = (bf16[512,1280]{1,0:T(8,128)(2,1)}, bf16[512,1280]{1,0:T(8,128)(2,1)}, u32[]{:S(2)}, u32[]{:S(2)}) collective-permute-start(bf16[512,1280]{1,0:T(8,128)(2,1)} %collective-permute-done.refs_14_.refs_9_.refs_11_), channel_id=1, source_target_pairs={{0,16},{16,32},{32,48},{48,0},{8,56},{24,8},{40,24},{56,40},{1,17}... | collective-permute-start | bytes 3932168 | tf_op jit(solution)/shard_map/ppermute | solution.py:23
  43.6 2.7 %fusion.13 = (bf16[512,1024]{1,0:T(8,128)(2,1)S(1)}, bf16[512,1024]{1,0:T(8,128)(2,1)}) fusion(bf16[1024,1024]{1,0:T(8,128)(2,1)} %collective-permute-done.3.refs_1_), kind=kLoop, calls=%fused_computation.40 | loop fusion | bytes 4194304 | tf_op jit(solution)/shard_map/slice | solution.py:225
  46.8 2.8 %collective-permute-start.8 = (bf16[512,1024]{1,0:T(8,128)(2,1)}, bf16[512,1024]{1,0:T(8,128)(2,1)S(1)}, u32[]{:S(2)}, u32[]{:S(2)}) collective-permute-start(bf16[512,1024]{1,0:T(8,128)(2,1)} %get-tuple-element.70), channel_id=1, source_target_pairs={{0,6},{2,0},{4,2},{6,4},{8,10},{10,12},{12,14},{14,8},{1,7},{3,1},... | collective-permute-start | bytes 3145736 | tf_op jit(solution)/shard_map/ppermute | solution.py:23
  50.6 2.1 %multiply_reduce_fusion = f32[1024]{0:T(1024)S(1)} fusion(bf16[1024,1024]{1,0:T(8,128)(2,1)} %collective-permute-done.3.refs_1_), kind=kLoop, calls=%fused_computation.1 | loop fusion | flops 3144704 | bytes 2101248 | tf_op jit(solution)/shard_map/reduce_sum | solution.py:32
  52.7 11.7 %pad_maximum_fusion = bf16[2048,1280]{1,0:T(8,128)(2,1)} fusion(bf16[512,1280]{1,0:T(8,128)(2,1)} %collective-permute-done.refs_14_.refs_9_.refs_11_, bf16[512,1280]{1,0:T(8,128)(2,1)S(1)} %collective-permute-done.2.refs_11_.refs_6_.refs_8_, bf16[512,1280]{1,0:T(8,128)(2,1)S(1)} %collective-permute-done.1.refs_9_.refs_4_.refs_6_, ...), kind=kLoop, calls=%fused_computation | loop fusion | flops 20971520 | bytes 10485760 | tf_op jit(solution)/shard_map/concatenate | solution.py:227
  64.3 8.5 %collective-permute-done.7.refs_2_ = bf16[512,1024]{1,0:T(8,128)(2,1)S(1)} collective-permute-done((bf16[512,1024]{1,0:T(8,128)(2,1)S(1)}, bf16[512,1024]{1,0:T(8,128)(2,1)S(1)}, u32[]{:S(2)}, u32[]{:S(2)}) %collective-permute-start.7) | collective-permute-done | bytes 1048608 | tf_op jit(solution)/shard_map/ppermute | solution.py:23
  74.3 2.0 %collective-permute-start.12 = (bf16[512,1024]{1,0:T(8,128)(2,1)}, bf16[512,1024]{1,0:T(8,128)(2,1)}, u32[]{:S(2)}, u32[]{:S(2)}) collective-permute-start(bf16[512,1024]{1,0:T(8,128)(2,1)} %get-tuple-element.68), channel_id=1, source_target_pairs={{0,2},{2,4},{4,6},{6,0},{8,14},{10,8},{12,10},{14,12},{1,3},{3,5},... | collective-permute-start | bytes 3145736 | tf_op jit(solution)/shard_map/ppermute | solution.py:23
  77.7 2.0 %collective-permute-start.11 = (bf16[512,1280]{1,0:T(8,128)(2,1)}, bf16[512,1280]{1,0:T(8,128)(2,1)}, u32[]{:S(2)}, u32[]{:S(2)}) collective-permute-start(bf16[512,1280]{1,0:T(8,128)(2,1)} %collective-permute-done.6.refs_15_.refs_10_.refs_12_), channel_id=1, source_target_pairs={{0,16},{16,32},{32,48},{48,0},{8,56},{24,8},{40,24},{56,40},{1,17}... | collective-permute-start | bytes 3932168 | tf_op jit(solution)/shard_map/ppermute | solution.py:23
  83.9 6.7 %collective-permute-done.12.refs_3_ = bf16[512,1024]{1,0:T(8,128)(2,1)} collective-permute-done((bf16[512,1024]{1,0:T(8,128)(2,1)}, bf16[512,1024]{1,0:T(8,128)(2,1)}, u32[]{:S(2)}, u32[]{:S(2)}) %collective-permute-start.12) | collective-permute-done | bytes 1048608 | tf_op jit(solution)/shard_map/ppermute | solution.py:23
  93.6 11.8 %collective-permute-done.13.refs_7_ = bf16[512,1024]{1,0:T(8,128)(2,1)} collective-permute-done((bf16[512,1024]{1,0:T(8,128)(2,1)}, bf16[512,1024]{1,0:T(8,128)(2,1)}, u32[]{:S(2)}, u32[]{:S(2)}) %collective-permute-start.13) | collective-permute-done | bytes 1048608 | tf_op jit(solution)/shard_map/ppermute | solution.py:27
  105.4 1.6 collective-permute-done.14.refs_0_
  107.0 2.7 %collective-permute-done.10.refs_17_.refs_12_.refs_14_ = bf16[512,1280]{1,0:T(8,128)(2,1)} collective-permute-done((bf16[512,1280]{1,0:T(8,128)(2,1)}, bf16[512,1280]{1,0:T(8,128)(2,1)}, u32[]{:S(2)}, u32[]{:S(2)}) %collective-permute-start.10) | collective-permute-done | bytes 1310752 | tf_op jit(solution)/shard_map/ppermute | solution.py:23
  112.1 2.5 %collective-permute-start.17 = (bf16[512,1024]{1,0:T(8,128)(2,1)}, bf16[512,1024]{1,0:T(8,128)(2,1)}, u32[]{:S(2)}, u32[]{:S(2)}) collective-permute-start(bf16[512,1024]{1,0:T(8,128)(2,1)} %collective-permute-done.9.refs_6_), channel_id=1, source_target_pairs={{0,6},{2,0},{4,2},{6,4},{8,10},{10,12},{12,14},{14,8},{1,7},{3,1},... | collective-permute-start | bytes 3145736 | tf_op jit(solution)/shard_map/ppermute | solution.py:23
  119.9 1.6 copy-done.18
  121.5 20.0 %shard_map.136.refs_15_.refs_17_ = f32[1024,1280]{1,0:T(8,128)} custom-call(s32[10]{0:T(128)} %add.125.sel_ref, bf16[1024,1024]{1,0:T(8,128)(2,1)} %refs_0_, bf16[1024,1024]{1,0:T(8,128)(2,1)} %collective-permute-done.3.refs_1_, bf16[512,1024]{1,0:T(8,128)(2,1)} %copy-done.8, bf16[512,1024]{1,0:T(8,128)(2,1)} %collective-permute-done.12.refs_3_, ...), custom_call_target="tpu_custom_call" | custom-call | flops 13421772800 | bytes 20000000 | tf_op jit(solution)/shard_map/pallas_call | solution.py:181
  142.0 2.5 %collective-permute-done.19.refs_1_ = bf16[256,1024]{1,0:T(8,128)(2,1)S(1)} collective-permute-done((bf16[256,1024]{1,0:T(8,128)(2,1)S(1)}, bf16[256,1024]{1,0:T(8,128)(2,1)S(1)}, u32[]{:S(2)}, u32[]{:S(2)}) %collective-permute-start.19) | collective-permute-done | bytes 524320 | tf_op jit(solution)/shard_map/ppermute | solution.py:23
  146.5 3.2 %collective-permute-start.24 = (bf16[256,1024]{1,0:T(8,128)(2,1)S(1)}, bf16[256,1024]{1,0:T(8,128)(2,1)S(1)}, u32[]{:S(2)}, u32[]{:S(2)}) collective-permute-start(bf16[256,1024]{1,0:T(8,128)(2,1)S(1)} %slice.36), channel_id=1, source_target_pairs={{0,6},{2,0},{4,2},{6,4},{8,10},{10,12},{12,14},{14,8},{1,7},{3,1},... | collective-permute-start | bytes 1572872 | tf_op jit(solution)/shard_map/ppermute | solution.py:23
  150.9 12.2 %shard_map.137.refs_20_ = bf16[1024,1024]{1,0:T(8,128)(2,1)} custom-call(s32[6]{0:T(128)} %add.132.sel_ref, bf16[512,1024]{1,0:T(8,128)(2,1)} %collective-permute-done.14.refs_0_, bf16[512,1024]{1,0:T(8,128)(2,1)} %collective-permute-done.16.refs_1_, bf16[512,1024]{1,0:T(8,128)(2,1)} %collective-permute-done.17.refs_2_, bf16[512,1280]{1,0:T(8,128)(2,1)} %copy-done.1, ...), custom_call_target="tpu_custom_call" | custom-call | flops 10026531840 | bytes 12000000 | tf_op jit(solution)/shard_map/pallas_call | solution.py:181
  164.3 12.1 %shard_map.138 = bf16[1024,1024]{1,0:T(8,128)(2,1)} custom-call(s32[6]{0:T(128)} %add.139.sel_ref, bf16[512,1024]{1,0:T(8,128)(2,1)} %collective-permute-done.20.refs_0_, bf16[256,1024]{1,0:T(8,128)(2,1)} %copy-done.21, bf16[256,1024]{1,0:T(8,128)(2,1)} %copy-done.23, bf16[256,1024]{1,0:T(8,128)(2,1)} %copy-done.24, ...), custom_call_target="tpu_custom_call", output_to_operand_aliasing={{}: (21, {})} | custom-call | flops 10026531840 | bytes 12000000 | tf_op jit(solution)/shard_map/pallas_call | solution.py:181
  (118 shorter events, 34.9 us)
Async XLA Ops:
  0.0 40.6 %collective-permute-start.3 = (bf16[1024,1024]{1,0:T(8,128)(2,1)}, bf16[1024,1024]{1,0:T(8,128)(2,1)}, u32[]{:S(2)}, u32[]{:S(2)}) collective-permute-start(bf16[1024,1024]{1,0:T(8,128)(2,1)} %refs_0_), channel_id=1, source_target_pairs={{0,2},{2,4},{4,6},{6,0},{8,14},{10,8},{12,10},{14,12},{1,3},{3,5},... | collective-permute-start | bytes 6291464 | tf_op jit(solution)/shard_map/ppermute | solution.py:23
  4.9 33.4 %collective-permute-start = (bf16[512,1280]{1,0:T(8,128)(2,1)S(1)}, bf16[512,1280]{1,0:T(8,128)(2,1)}, u32[]{:S(2)}, u32[]{:S(2)}) collective-permute-start(bf16[512,1280]{1,0:T(8,128)(2,1)S(1)} %multiply_convert_fusion.refs_8_.refs_3_.refs_5_), channel_id=1, source_target_pairs={{0,64},{64,0},{1,65},{65,1},{2,66},{66,2},{3,67},{67,3},{4,68},{68... | collective-permute-start | bytes 3932168 | tf_op jit(solution)/shard_map/ppermute | solution.py:27
  8.9 30.6 %collective-permute-start.1 = (bf16[512,1280]{1,0:T(8,128)(2,1)S(1)}, bf16[512,1280]{1,0:T(8,128)(2,1)S(1)}, u32[]{:S(2)}, u32[]{:S(2)}) collective-permute-start(bf16[512,1280]{1,0:T(8,128)(2,1)S(1)} %multiply_convert_fusion.refs_8_.refs_3_.refs_5_), channel_id=1, source_target_pairs={{0,16},{16,32},{32,48},{48,0},{8,56},{24,8},{40,24},{56,40},{1,17}... | collective-permute-start | bytes 3932168 | tf_op jit(solution)/shard_map/ppermute | solution.py:23
  10.4 30.2 %collective-permute-start.2 = (bf16[512,1280]{1,0:T(8,128)(2,1)S(1)}, bf16[512,1280]{1,0:T(8,128)(2,1)S(1)}, u32[]{:S(2)}, u32[]{:S(2)}) collective-permute-start(bf16[512,1280]{1,0:T(8,128)(2,1)S(1)} %multiply_convert_fusion.refs_8_.refs_3_.refs_5_), channel_id=1, source_target_pairs={{0,48},{16,0},{32,16},{48,32},{8,24},{24,40},{40,56},{56,8},{1,49}... | collective-permute-start | bytes 3932168 | tf_op jit(solution)/shard_map/ppermute | solution.py:23
  13.3 23.7 %collective-permute-start.4 = (bf16[512,1024]{1,0:T(8,128)(2,1)S(1)}, bf16[512,1024]{1,0:T(8,128)(2,1)S(1)}, u32[]{:S(2)}, u32[]{:S(2)}) collective-permute-start(bf16[512,1024]{1,0:T(8,128)(2,1)S(1)} %get-tuple-element.61), channel_id=1, source_target_pairs={{0,6},{2,0},{4,2},{6,4},{8,10},{10,12},{12,14},{14,8},{1,7},{3,1},... | collective-permute-start | bytes 3145736 | tf_op jit(solution)/shard_map/ppermute | solution.py:23
  40.6 32.5 %collective-permute-start.5 = (bf16[512,1280]{1,0:T(8,128)(2,1)S(1)}, bf16[512,1280]{1,0:T(8,128)(2,1)S(1)}, u32[]{:S(2)}, u32[]{:S(2)}) collective-permute-start(bf16[512,1280]{1,0:T(8,128)(2,1)S(1)} %collective-permute-done.1.refs_9_.refs_4_.refs_6_), channel_id=1, source_target_pairs={{0,16},{16,32},{32,48},{48,0},{8,56},{24,8},{40,24},{56,40},{1,17}... | collective-permute-start | bytes 3932168 | tf_op jit(solution)/shard_map/ppermute | solution.py:23
  41.8 32.5 %collective-permute-start.6 = (bf16[512,1280]{1,0:T(8,128)(2,1)}, bf16[512,1280]{1,0:T(8,128)(2,1)}, u32[]{:S(2)}, u32[]{:S(2)}) collective-permute-start(bf16[512,1280]{1,0:T(8,128)(2,1)} %collective-permute-done.refs_14_.refs_9_.refs_11_), channel_id=1, source_target_pairs={{0,16},{16,32},{32,48},{48,0},{8,56},{24,8},{40,24},{56,40},{1,17}... | collective-permute-start | bytes 3932168 | tf_op jit(solution)/shard_map/ppermute | solution.py:23
  46.3 26.6 %collective-permute-start.7 = (bf16[512,1024]{1,0:T(8,128)(2,1)S(1)}, bf16[512,1024]{1,0:T(8,128)(2,1)S(1)}, u32[]{:S(2)}, u32[]{:S(2)}) collective-permute-start(bf16[512,1024]{1,0:T(8,128)(2,1)S(1)} %get-tuple-element.113), channel_id=1, source_target_pairs={{0,2},{2,4},{4,6},{6,0},{8,14},{10,8},{12,10},{14,12},{1,3},{3,5},... | collective-permute-start | bytes 3145736 | tf_op jit(solution)/shard_map/ppermute | solution.py:23
  46.8 26.1 %collective-permute-start.8 = (bf16[512,1024]{1,0:T(8,128)(2,1)}, bf16[512,1024]{1,0:T(8,128)(2,1)S(1)}, u32[]{:S(2)}, u32[]{:S(2)}) collective-permute-start(bf16[512,1024]{1,0:T(8,128)(2,1)} %get-tuple-element.70), channel_id=1, source_target_pairs={{0,6},{2,0},{4,2},{6,4},{8,10},{10,12},{12,14},{14,8},{1,7},{3,1},... | collective-permute-start | bytes 3145736 | tf_op jit(solution)/shard_map/ppermute | solution.py:23
  49.5 23.5 %collective-permute-start.9 = (bf16[512,1024]{1,0:T(8,128)(2,1)S(1)}, bf16[512,1024]{1,0:T(8,128)(2,1)}, u32[]{:S(2)}, u32[]{:S(2)}) collective-permute-start(bf16[512,1024]{1,0:T(8,128)(2,1)S(1)} %get-tuple-element.61), channel_id=1, source_target_pairs={{0,1},{1,0},{2,3},{3,2},{4,5},{5,4},{6,7},{7,6},{8,9},{9,8},{10,11... | collective-permute-start | bytes 3145736 | tf_op jit(solution)/shard_map/ppermute | solution.py:27
  74.3 35.4 %collective-permute-start.15 = (bf16[2048,1280]{1,0:T(8,128)(2,1)}, bf16[2048,1280]{1,0:T(8,128)(2,1)}, u32[]{:S(2)}, u32[]{:S(2)}) collective-permute-start(bf16[2048,1280]{1,0:T(8,128)(2,1)} %pad_maximum_fusion), channel_id=1, source_target_pairs={{0,8},{8,0},{1,9},{9,1},{2,10},{10,2},{3,11},{11,3},{4,12},{12,4},... | collective-permute-start | bytes 15728648 | tf_op jit(solution)/shard_map/ppermute | solution.py:27
  74.3 16.4 %collective-permute-start.12 = (bf16[512,1024]{1,0:T(8,128)(2,1)}, bf16[512,1024]{1,0:T(8,128)(2,1)}, u32[]{:S(2)}, u32[]{:S(2)}) collective-permute-start(bf16[512,1024]{1,0:T(8,128)(2,1)} %get-tuple-element.68), channel_id=1, source_target_pairs={{0,2},{2,4},{4,6},{6,0},{8,14},{10,8},{12,10},{14,12},{1,3},{3,5},... | collective-permute-start | bytes 3145736 | tf_op jit(solution)/shard_map/ppermute | solution.py:23
  77.7 32.0 %collective-permute-start.10 = (bf16[512,1280]{1,0:T(8,128)(2,1)}, bf16[512,1280]{1,0:T(8,128)(2,1)}, u32[]{:S(2)}, u32[]{:S(2)}) collective-permute-start(bf16[512,1280]{1,0:T(8,128)(2,1)} %collective-permute-done.refs_14_.refs_9_.refs_11_), channel_id=1, source_target_pairs={{0,48},{16,0},{32,16},{48,32},{8,24},{24,40},{40,56},{56,8},{1,49}... | collective-permute-start | bytes 3932168 | tf_op jit(solution)/shard_map/ppermute | solution.py:23
  77.7 31.9 %collective-permute-start.11 = (bf16[512,1280]{1,0:T(8,128)(2,1)}, bf16[512,1280]{1,0:T(8,128)(2,1)}, u32[]{:S(2)}, u32[]{:S(2)}) collective-permute-start(bf16[512,1280]{1,0:T(8,128)(2,1)} %collective-permute-done.6.refs_15_.refs_10_.refs_12_), channel_id=1, source_target_pairs={{0,16},{16,32},{32,48},{48,0},{8,56},{24,8},{40,24},{56,40},{1,17}... | collective-permute-start | bytes 3932168 | tf_op jit(solution)/shard_map/ppermute | solution.py:23
  79.8 25.7 %collective-permute-start.13 = (bf16[512,1024]{1,0:T(8,128)(2,1)}, bf16[512,1024]{1,0:T(8,128)(2,1)}, u32[]{:S(2)}, u32[]{:S(2)}) collective-permute-start(bf16[512,1024]{1,0:T(8,128)(2,1)} %get-tuple-element.70), channel_id=1, source_target_pairs={{0,1},{1,0},{2,3},{3,2},{4,5},{5,4},{6,7},{7,6},{8,9},{9,8},{10,11... | collective-permute-start | bytes 3145736 | tf_op jit(solution)/shard_map/ppermute | solution.py:27
  90.7 16.3 %collective-permute-start.14 = (bf16[512,1024]{1,0:T(8,128)(2,1)}, bf16[512,1024]{1,0:T(8,128)(2,1)}, u32[]{:S(2)}, u32[]{:S(2)}) collective-permute-start(bf16[512,1024]{1,0:T(8,128)(2,1)} %collective-permute-done.9.refs_6_), channel_id=1, source_target_pairs={{0,2},{2,4},{4,6},{6,0},{8,14},{10,8},{12,10},{14,12},{1,3},{3,5},... | collective-permute-start | bytes 3145736 | tf_op jit(solution)/shard_map/ppermute | solution.py:23
  109.7 10.2 %collective-permute-start.21 = (bf16[1024,1280]{1,0:T(8,128)(2,1)S(1)}, bf16[1024,1280]{1,0:T(8,128)(2,1)S(1)}, u32[]{:S(2)}, u32[]{:S(2)}) collective-permute-start(bf16[1024,1280]{1,0:T(8,128)(2,1)S(1)} %pad_maximum_fusion.1), channel_id=1, source_target_pairs={{0,8},{8,0},{1,9},{9,1},{2,10},{10,2},{3,11},{11,3},{4,12},{12,4},... | collective-permute-start | bytes 7864328 | tf_op jit(solution)/shard_map/ppermute | solution.py:27
  111.4 30.2 %collective-permute-start.16 = (bf16[512,1024]{1,0:T(8,128)(2,1)}, bf16[512,1024]{1,0:T(8,128)(2,1)}, u32[]{:S(2)}, u32[]{:S(2)}) collective-permute-start(bf16[512,1024]{1,0:T(8,128)(2,1)} %collective-permute-done.14.refs_0_), channel_id=1, source_target_pairs={{0,2},{2,4},{4,6},{6,0},{8,14},{10,8},{12,10},{14,12},{1,3},{3,5},... | collective-permute-start | bytes 3145736 | tf_op jit(solution)/shard_map/ppermute | solution.py:23
  112.1 29.4 %collective-permute-start.17 = (bf16[512,1024]{1,0:T(8,128)(2,1)}, bf16[512,1024]{1,0:T(8,128)(2,1)}, u32[]{:S(2)}, u32[]{:S(2)}) collective-permute-start(bf16[512,1024]{1,0:T(8,128)(2,1)} %collective-permute-done.9.refs_6_), channel_id=1, source_target_pairs={{0,6},{2,0},{4,2},{6,4},{8,10},{10,12},{12,14},{14,8},{1,7},{3,1},... | collective-permute-start | bytes 3145736 | tf_op jit(solution)/shard_map/ppermute | solution.py:23
  117.3 24.7 %collective-permute-start.20 = (bf16[512,1024]{1,0:T(8,128)(2,1)S(1)}, bf16[512,1024]{1,0:T(8,128)(2,1)}, u32[]{:S(2)}, u32[]{:S(2)}) collective-permute-start(bf16[512,1024]{1,0:T(8,128)(2,1)S(1)} %copy-done.9), channel_id=1, source_target_pairs={{0,1},{1,0},{2,3},{3,2},{4,5},{5,4},{6,7},{7,6},{8,9},{9,8},{10,11... | collective-permute-start | bytes 3145736 | tf_op jit(solution)/shard_map/ppermute | solution.py:27
  118.8 25.7 %collective-permute-start.19 = (bf16[256,1024]{1,0:T(8,128)(2,1)S(1)}, bf16[256,1024]{1,0:T(8,128)(2,1)S(1)}, u32[]{:S(2)}, u32[]{:S(2)}) collective-permute-start(bf16[256,1024]{1,0:T(8,128)(2,1)S(1)} %slice.36), channel_id=1, source_target_pairs={{0,2},{2,4},{4,6},{6,0},{8,14},{10,8},{12,10},{14,12},{1,3},{3,5},... | collective-permute-start | bytes 1572872 | tf_op jit(solution)/shard_map/ppermute | solution.py:23
  146.5 16.6 %collective-permute-start.23 = (bf16[256,1024]{1,0:T(8,128)(2,1)S(1)}, bf16[256,1024]{1,0:T(8,128)(2,1)S(1)}, u32[]{:S(2)}, u32[]{:S(2)}) collective-permute-start(bf16[256,1024]{1,0:T(8,128)(2,1)S(1)} %collective-permute-done.19.refs_1_), channel_id=1, source_target_pairs={{0,2},{2,4},{4,6},{6,0},{8,14},{10,8},{12,10},{14,12},{1,3},{3,5},... | collective-permute-start | bytes 1572872 | tf_op jit(solution)/shard_map/ppermute | solution.py:23
  146.5 16.7 %collective-permute-start.24 = (bf16[256,1024]{1,0:T(8,128)(2,1)S(1)}, bf16[256,1024]{1,0:T(8,128)(2,1)S(1)}, u32[]{:S(2)}, u32[]{:S(2)}) collective-permute-start(bf16[256,1024]{1,0:T(8,128)(2,1)S(1)} %slice.36), channel_id=1, source_target_pairs={{0,6},{2,0},{4,2},{6,4},{8,10},{10,12},{12,14},{14,8},{1,7},{3,1},... | collective-permute-start | bytes 1572872 | tf_op jit(solution)/shard_map/ppermute | solution.py:23
  149.7 13.4 %collective-permute-start.25 = (bf16[256,1024]{1,0:T(8,128)(2,1)S(1)}, bf16[256,1024]{1,0:T(8,128)(2,1)S(1)}, u32[]{:S(2)}, u32[]{:S(2)}) collective-permute-start(bf16[256,1024]{1,0:T(8,128)(2,1)S(1)} %slice.37), channel_id=1, source_target_pairs={{0,1},{1,0},{2,3},{3,2},{4,5},{5,4},{6,7},{7,6},{8,9},{9,8},{10,11... | collective-permute-start | bytes 1572872 | tf_op jit(solution)/shard_map/ppermute | solution.py:27
  (28 other events, 315.3 us)
